TPU v7x, 32 devices: a whole 2x2x4 slice. The times are simulated.
32 devices in a mesh: region: 8 (over z, y), angle: 4 (over x, core).
Axes of the slice: x: 2, y: 2, z: 4, core: 2. Of those that a mesh axis runs over, the one named last changes fastest.
Arguments:
- volume: float32 [128, 128, 128], P('region'), may hold values from -6 to 6
- blocks: bfloat16 [8192, 128, 128], P(('region', 'angle')), may hold values from -0.1875 to 0.1875
- tile_of: int32 [8192], P(('region', 'angle')), may hold values from 0 to 15
- slot_of: int32 [8192], P(('region', 'angle')), may hold values from 0 to 7
- live_count: int32 [32], P(('region', 'angle')), may hold values from 96 to 256, as said below
- ray_of: int32 [256], P(('region', 'angle')), may hold values from 0 to 7
- sinogram: float32 [256, 128, 128], P(('region', 'angle')), may hold values from -6 to 6
- ray_weight: float32 [256, 128], P(('region', 'angle')), may hold values from 0.5 to 2
- pixel_weight: float32 [128, 128], P('region'), may hold values from 0.1 to 0.5
Outputs:
- updated: float32 [128, 128, 128], P(('region', 'angle'))
- residual: float32 [256, 128, 128], P(('region', 'angle'))
Inputs may be any that keep to these rules, and one draw needn't show every extreme that they name: Blocks at positions 256 * d + j with j < live_count[d] are in use, the others are ignored; every device uses at least 96 blocks, and some device uses all 256.
All inputs are finite; a program needn't handle non-finite values.
Results may differ from a plain program's by a relative error of at most 0.0039.
Values may be sent and summed in bfloat16 or wider, within the bound.
No kernel may reach another device: no remote copies, remote signals or barrier semaphores. Data moves between devices by JAX's collectives and lax.ppermute only.
A program may use at most 128 MiB of HBM per device.

v0:
```python
import jax
import jax.numpy as jnp
from jax import lax
from jax.sharding import PartitionSpec as P


def body(volume, blocks, tile_of, slot_of, live_count, ray_of, sinogram, ray_weight, pixel_weight):
    n_region = lax.axis_size("region")
    n_angle = lax.axis_size("angle")
    slot_count = ray_of.shape[0]
    capacity = slot_count // n_region
    ray_rows = sinogram.shape[0]
    tile_rows = volume.shape[0]
    entries = blocks.shape[0]
    is_live = jnp.arange(entries, dtype=jnp.int32) < live_count[0]
    volume_b = volume.astype(jnp.bfloat16)
    picked = volume_b[tile_of]
    forward = jnp.einsum("esp,erp->esr", picked, blocks, preferred_element_type=jnp.float32)
    slot_ids = jnp.where(is_live, slot_of, slot_count)
    partial_value = jax.ops.segment_sum(forward, slot_ids, num_segments=slot_count + 1)[:slot_count]
    received = lax.all_to_all(
        partial_value.reshape((n_region, capacity) + partial_value.shape[1:]),
        "region",
        split_axis=0,
        concat_axis=0,
        tiled=True,
    )
    projection = jax.ops.segment_sum(
        received.reshape(partial_value.shape), ray_of, num_segments=ray_rows
    )
    residual = ray_weight[:, None, :] * (sinogram - projection)
    residual_b = residual.astype(jnp.bfloat16)
    outgoing = residual_b[ray_of].reshape((n_region, capacity) + residual_b.shape[1:])
    returned = lax.all_to_all(outgoing, "region", split_axis=0, concat_axis=0, tiled=True).reshape(
        (slot_count,) + residual_b.shape[1:]
    )
    slot_rows = returned[slot_of]
    backward = jnp.einsum("esr,erp->esp", slot_rows, blocks, preferred_element_type=jnp.float32)
    tile_ids = jnp.where(is_live, tile_of, tile_rows)
    gradient = jax.ops.segment_sum(backward, tile_ids, num_segments=tile_rows + 1)[:tile_rows]
    per_angle = tile_rows // n_angle
    first_tile = lax.axis_index("angle") * per_angle
    all_tiles = lax.psum(gradient, "angle")
    my_share = lax.dynamic_slice_in_dim(all_tiles, first_tile, per_angle, 0)
    volume_part = lax.dynamic_slice_in_dim(volume, first_tile, per_angle, 0)
    weight_part = lax.dynamic_slice_in_dim(pixel_weight, first_tile, per_angle, 0)
    updated = volume_part + weight_part[:, None, :] * my_share
    return (updated, residual)


def solution(mesh):
    placed = (
        P("region", None, None),
        P(("region", "angle"), None, None),
        P(("region", "angle")),
        P(("region", "angle")),
        P(("region", "angle")),
        P(("region", "angle")),
        P(("region", "angle"), None, None),
        P(("region", "angle"), None),
        P("region", None),
    )
    return jax.shard_map(
        body,
        mesh=mesh,
        in_specs=placed,
        out_specs=(P(("region", "angle"), None, None), P(("region", "angle"), None, None)),
        check_vma=False,
    )
```

profile of v0, /device:TPU:0, one launch (start us, length us, event | category | flops | bytes accessed | tf_op | source)
XLA Modules:
  0.0 208.3 jit_solution(4568498242971905080)
XLA Ops:
  7.2 0.0 copy-start
  7.8 0.7 compare_select_fusion
  8.5 1.3 convert_element_type.6
  9.9 8.6 %gather_fusion = bf16[256,128,128]{2,1,0:T(8,128)(2,1)} fusion(bf16[16,128,128]{2,1,0:T(8,128)(2,1)S(1)} %convert_element_type.6, s32[1024]{0:T(1024)S(1)} %pad_clamp_fusion.2), kind=kCustom, calls=%fused_computation | custom fusion | bytes 16778240 | tf_op jit(solution)/shard_map/gather | solution.py:17
  18.4 17.4 %fusion.3 = f32[256,128,128]{2,1,0:T(8,128)} fusion(bf16[256,128,128]{2,1,0:T(8,128)(2,1)} %gather_fusion, bf16[256,128,128]{2,1,0:T(8,128)(2,1)} %param.10), kind=kOutput, calls=%fused_computation.20 | convolution fusion | flops 1073741824 | bytes 33554432 | tf_op jit(solution)/shard_map/esp,erp->esr/dot_general | solution.py:18
  35.9 0.0 copy-start.3
  35.9 33.1 %scatter_fusion = f32[9,128,128]{2,1,0:T(8,128)S(1)} fusion(f32[9,128,128]{2,1,0:T(8,128)S(1)} %broadcast_in_dim.41, s32[256]{0:T(256)S(1)} %get-tuple-element.5, f32[256,128,128]{2,1,0:T(8,128)} %fusion.3), kind=kCustom, calls=%fused_computation.3 | custom fusion | flops 4194304 | bytes 50332672 | tf_op jit(solution)/shard_map/scatter-add | solution.py:20
  69.1 0.8 slice_bitcast_fusion
  69.9 7.3 %all-to-all-start = ((f32[8,1,128,128]{3,2,1,0:T(8,128)}), f32[8,1,128,128]{3,2,1,0:T(8,128)S(1)}, u32[]{:S(2)}, u32[]{:S(2)}) async-start(f32[8,1,128,128]{3,2,1,0:T(8,128)} %slice_bitcast_fusion), calls=%async_computation | async-start | bytes 1048576 | tf_op jit(solution)/shard_map/all_to_all | solution.py:21
  77.2 14.5 %all-to-all-done = f32[8,1,128,128]{3,2,1,0:T(8,128)S(1)} async-done(((f32[8,1,128,128]{3,2,1,0:T(8,128)}), f32[8,1,128,128]{3,2,1,0:T(8,128)S(1)}, u32[]{:S(2)}, u32[]{:S(2)}) %all-to-all-start) | async-done | bytes 524320 | tf_op jit(solution)/shard_map/all_to_all | solution.py:21
  91.7 1.0 scatter_fusion.1
  92.8 0.9 fusion.2
  93.7 1.3 gather_fusion.1
  95.0 3.6 %all-to-all-start.1 = ((bf16[8,1,128,128]{3,2,1,0:T(8,128)(2,1)}), bf16[8,1,128,128]{3,2,1,0:T(8,128)(2,1)S(1)}, u32[]{:S(2)}, u32[]{:S(2)}) async-start(bf16[8,1,128,128]{3,2,1,0:T(8,128)(2,1)} %bitcast.4), calls=%async_computation.1 | async-start | bytes 524288 | tf_op jit(solution)/shard_map/all_to_all | solution.py:34
  98.6 0.2 all-reduce.2.cloned.1.call-start
  98.8 8.9 %all-to-all-done.1 = bf16[8,1,128,128]{3,2,1,0:T(8,128)(2,1)S(1)} async-done(((bf16[8,1,128,128]{3,2,1,0:T(8,128)(2,1)}), bf16[8,1,128,128]{3,2,1,0:T(8,128)(2,1)S(1)}, u32[]{:S(2)}, u32[]{:S(2)}) %all-to-all-start.1) | async-done | bytes 262176 | tf_op jit(solution)/shard_map/all_to_all | solution.py:34
  107.7 8.6 %gather_fusion.2 = bf16[256,128,128]{2,1,0:T(8,128)(2,1)} fusion(bf16[8,128,128]{2,1,0:T(8,128)(2,1)S(1)} %bitcast.13, s32[1024]{0:T(1024)S(1)} %pad_clamp_fusion), kind=kCustom, calls=%fused_computation.2 | custom fusion | bytes 16778240 | tf_op jit(solution)/shard_map/gather | solution.py:37
  116.2 13.8 %fusion.4 = f32[256,128,128]{2,1,0:T(8,128)} fusion(bf16[256,128,128]{2,1,0:T(8,128)(2,1)} %gather_fusion.2, bf16[256,128,128]{2,1,0:T(8,128)(2,1)} %param.10), kind=kOutput, calls=%fused_computation.21 | convolution fusion | flops 1073741824 | bytes 33554432 | tf_op jit(solution)/shard_map/esr,erp->esp/dot_general | solution.py:38
  130.1 0.1 broadcast_in_dim.36
  130.2 33.2 %scatter_fusion.2 = f32[17,128,128]{2,1,0:T(8,128)S(1)} fusion(f32[17,128,128]{2,1,0:T(8,128)S(1)} %broadcast_in_dim.36, s32[256]{0:T(256)S(1)} %get-tuple-element.8, f32[256,128,128]{2,1,0:T(8,128)} %fusion.4), kind=kCustom, calls=%fused_computation.5 | custom fusion | flops 4194304 | bytes 50332672 | tf_op jit(solution)/shard_map/scatter-add | solution.py:40
  163.4 1.1 slice.15
  164.5 0.0 all-reduce.2.cloned.1.call-update
  164.5 35.2 %all-reduce.2.cloned.1.call-done = f32[16,128,128]{2,1,0:T(8,128)} async-done(((f32[16,128,128]{2,1,0:T(8,128)}), f32[16,128,128]{2,1,0:T(8,128)}) %all-reduce.2.cloned.1.call-update) | async-done | bytes 1048592 | tf_op jit(solution)/shard_map/psum | solution.py:43
  199.7 1.8 multiply_add_fusion
  (13 shorter events, 0.1 us)
Async XLA Ops:
  7.2 157.3 %copy-start = (f32[16,128]{1,0:T(8,128)S(1)}, f32[16,128]{1,0:T(8,128)}, u32[]{:S(2)}) copy-start(f32[16,128]{1,0:T(8,128)} %param.17) | copy-start | bytes 24580
  35.9 41.3 %copy-start.3 = (s32[8]{0:T(128)S(1)}, s32[8]{0:T(128)}, u32[]{:S(2)}) copy-start(s32[8]{0:T(128)} %param.14) | copy-start | bytes 100
  35.9 56.9 %copy-start.1 = (f32[8,128,128]{2,1,0:T(8,128)S(1)}, f32[8,128,128]{2,1,0:T(8,128)}, u32[]{:S(2)}) copy-start(f32[8,128,128]{2,1,0:T(8,128)} %param.15) | copy-start | bytes 1572868
  35.9 56.9 %copy-start.2 = (f32[8,128]{1,0:T(8,128)S(1)}, f32[8,128]{1,0:T(8,128)}, u32[]{:S(2)}) copy-start(f32[8,128]{1,0:T(8,128)} %param.16) | copy-start | bytes 12292
  69.9 21.8 %all-to-all-start = ((f32[8,1,128,128]{3,2,1,0:T(8,128)}), f32[8,1,128,128]{3,2,1,0:T(8,128)S(1)}, u32[]{:S(2)}, u32[]{:S(2)}) async-start(f32[8,1,128,128]{3,2,1,0:T(8,128)} %slice_bitcast_fusion), calls=%async_computation | async-start | bytes 1048576 | tf_op jit(solution)/shard_map/all_to_all | solution.py:21
  95.0 12.7 %all-to-all-start.1 = ((bf16[8,1,128,128]{3,2,1,0:T(8,128)(2,1)}), bf16[8,1,128,128]{3,2,1,0:T(8,128)(2,1)S(1)}, u32[]{:S(2)}, u32[]{:S(2)}) async-start(bf16[8,1,128,128]{3,2,1,0:T(8,128)(2,1)} %bitcast.4), calls=%async_computation.1 | async-start | bytes 524288 | tf_op jit(solution)/shard_map/all_to_all | solution.py:34
  98.6 101.1 %all-reduce.2.cloned.1.call-start = ((), (), s32[]{:S(2)}) async-start(), calls=%async_computation.2 | async-start | bytes 2097152 | tf_op jit(solution)/shard_map/psum | solution.py:43
Sparse Core Ops, SparseCore 0:
  164.6 35.0 all-reduce.1
where the time goes:
time: 210 us; the launch traced here: 208 us
  other arithmetic  72 us (34%)
  waiting for transfers between devices  58.6 us (28%)
  matrix products  31.2 us (15%)
  local copies, waits for them, and re-layouts  20.5 us (10%)
  between operations  14.8 us (7%)
  starting transfers between devices  11.1 us (5%)
    psum x1, waiting for transfers between devices, body(): all_tiles = lax.psum(gradient, 'angle')  35.2 us
    scatter-add x1, other arithmetic, body(): jax.ops.segment_sum(backward, tile_ids, num_segments=tile_rows + 1)  33.2 us
    scatter-add x1, other arithmetic, body(): jax.ops.segment_sum(forward, slot_ids, num_segments=slot_count + 1)  33.1 us
    dot_general x1, matrix products, body(): jnp.einsum('esp,erp->esr', picked, blocks, preferred_element_type=jnp.flo...  17.4 us
    all_to_all x1, waiting for transfers between devices, body(): lax.all_to_all(partial_value.reshape((n_region, capacity) + partial_value...  14.5 us
    dot_general x1, matrix products, body(): jnp.einsum('esr,erp->esp', slot_rows, blocks, preferred_element_type=jnp....  13.8 us
    all_to_all x1, waiting for transfers between devices, body(): lax.all_to_all(outgoing, 'region', split_axis=0, concat_axis=0, tiled=True)  8.86 us
    gather x1, local copies, waits for them, and re-layouts, body(): picked = volume_b[tile_of]  8.57 us
  transfers between devices with their start and end apart: 3, of which 3 were waited for; matrix products, arithmetic and copies ran while one was open for 0% of the time, Pallas kernels for 0%

commit v1 on v0

v1 whole, which is shorter than its diff:
```python
import functools

import jax
import jax.numpy as jnp
from jax import lax
from jax.experimental import pallas as pl
from jax.experimental.pallas import tpu as pltpu
from jax.sharding import PartitionSpec as P

CHUNKS = 8
UNROLL = 8
VMEM_LIMIT = 40 * 1024 * 1024
SMEM_SPEC = pl.BlockSpec(memory_space=pltpu.SMEM)
VMEM_SPEC = pl.BlockSpec(memory_space=pltpu.VMEM)
ANY_SPEC = pl.BlockSpec(memory_space=pl.ANY)


def dot_pair(x, y, dims):
    return lax.dot_general(x, y, (dims, ((), ())), preferred_element_type=jnp.float32)


def forward_kernel(per_angle, tile_of, slot_of, live_count, volume, blocks, partial_out, held, back_first, back_second,
                   back_count, volume_b, total, first, second, open_slot, open_tile, sems):
    entries = blocks.shape[0]
    slot_count, tile_rows = partial_out.shape[0], volume.shape[0]
    groups = back_count.shape[0]
    room = back_first.shape[0] // groups
    chunk = entries // CHUNKS
    copies = [
        pltpu.make_async_copy(blocks.at[pl.ds(c * chunk, chunk)], held.at[pl.ds(c * chunk, chunk)], sems.at[c])
        for c in range(CHUNKS)
    ]
    for copy in copies:
        copy.start()
    held[entries] = jnp.zeros(held.shape[1:], held.dtype)
    volume_b[...] = volume[...].astype(jnp.bfloat16)
    total[...] = jnp.zeros_like(total)
    for s in range(slot_count):
        open_slot[s] = -1
    for t in range(tile_rows):
        open_tile[t] = -1
    for g in range(groups):
        back_count[g] = 0
    live = live_count[0]

    def place(e, n):
        s = slot_of[e]
        t = tile_of[e]
        is_live = e < live
        p = open_slot[s]
        first[n] = p
        second[n] = e
        paired = jnp.logical_and(p >= 0, is_live)
        open_slot[s] = jnp.where(is_live, jnp.where(p >= 0, -1, e), p)
        q = open_tile[t]
        g = lax.div(t, per_angle)
        m = back_count[g]
        back_first[g * room + m] = q
        back_second[g * room + m] = e
        back_count[g] = m + jnp.where(jnp.logical_and(q >= 0, is_live), 1, 0)
        open_tile[t] = jnp.where(is_live, jnp.where(q >= 0, -1, e), q)
        return n + jnp.where(paired, 1, 0)

    def multiply(i, _):
        for u in range(UNROLL):
            j = i * UNROLL + u
            a, b = first[j], second[j]
            ka, kb = jnp.minimum(a, entries - 1), jnp.minimum(b, entries - 1)
            s = slot_of[ka]
            left = jnp.concatenate([volume_b[tile_of[ka]], volume_b[tile_of[kb]]], axis=1)
            right = jnp.concatenate([held[a], held[b]], axis=1)
            total[s] += dot_pair(left, right, ((1,), (1,)))
        return 0

    n, done = jnp.int32(0), jnp.int32(0)
    marks = []
    for c in range(CHUNKS):
        n = lax.fori_loop(c * chunk, (c + 1) * chunk, place, n, unroll=8)
        marks.append(n)
    for s in range(slot_count):
        p = open_slot[s]
        first[n] = p
        second[n] = entries
        n = n + jnp.where(p >= 0, 1, 0)
    for u in range(UNROLL):
        first[n + u] = entries
        second[n + u] = entries
    for t in range(tile_rows):
        p = open_tile[t]
        g = t // per_angle
        m = back_count[g]
        back_first[g * room + m] = p
        back_second[g * room + m] = entries
        back_count[g] = m + jnp.where(p >= 0, 1, 0)
    for g in range(groups):
        m = back_count[g]
        for u in range(UNROLL):
            back_first[g * room + m + u] = entries
            back_second[g * room + m + u] = entries
    for c in range(CHUNKS):
        copies[c].wait()
        if c == CHUNKS - 1:
            upto = lax.div(n + (UNROLL - 1), UNROLL)
        else:
            upto = lax.div(marks[c], UNROLL)
        lax.fori_loop(done, upto, multiply, 0)
        done = upto
    partial_out[...] = total[...].astype(partial_out.dtype)


def residual_kernel(ray_of, received, sinogram, ray_weight, residual, outgoing, total):
    total[...] = jnp.zeros_like(total)
    slot_count, ray_rows = received.shape[0], sinogram.shape[0]
    for r in range(slot_count):
        total[ray_of[r]] += received[r].astype(jnp.float32)
    residual[...] = ray_weight[...][:, None, :] * (sinogram[...] - total[...])
    for r in range(slot_count):
        outgoing[r] = residual[ray_of[r]].astype(outgoing.dtype)


def backward_sums(mask, per_angle, me, tile_of, slot_of, back_first, back_second, back_count, held, returned, total):
    entries = tile_of.shape[0]
    groups = back_count.shape[0]
    room = back_first.shape[0] // groups
    g = jnp.bitwise_xor(me[0], mask)
    total[...] = jnp.zeros_like(total)

    def multiply(i, _):
        for u in range(UNROLL):
            j = g * room + i * UNROLL + u
            a, b = back_first[j], back_second[j]
            ka, kb = jnp.minimum(a, entries - 1), jnp.minimum(b, entries - 1)
            t = lax.rem(tile_of[ka], per_angle)
            left = jnp.concatenate([returned[slot_of[ka]], returned[slot_of[kb]]], axis=1)
            right = jnp.concatenate([held[a], held[b]], axis=0)
            total[t] += dot_pair(left, right, ((1,), (0,)))
        return 0

    lax.fori_loop(0, lax.div(back_count[g] + (UNROLL - 1), UNROLL), multiply, 0)


def backward_kernel(mask, per_angle, n_recv, *refs):
    core, recv, (out, total) = refs[:8], refs[8:8 + n_recv], refs[8 + n_recv:]
    backward_sums(mask, per_angle, *core, total)
    value = total[...]
    for piece in recv:
        value = value + piece[...].astype(jnp.float32)
    out[...] = value.astype(out.dtype)


def update_kernel(mask, per_angle, n_recv, *refs):
    core, recv, (volume, weight, out, total) = refs[:8], refs[8:8 + n_recv], refs[8 + n_recv:]
    backward_sums(mask, per_angle, *core, total)
    value = total[...]
    for piece in recv:
        value = value + piece[...].astype(jnp.float32)
    out[...] = volume[...] + weight[...][:, None, :] * value


def body(volume, blocks, tile_of, slot_of, live_count, ray_of, sinogram, ray_weight, pixel_weight):
    n_region = lax.axis_size("region")
    n_angle = lax.axis_size("angle")
    slot_count = ray_of.shape[0]
    capacity = slot_count // n_region
    ray_rows = sinogram.shape[0]
    tile_rows, slices, pixels = volume.shape
    entries, rays, _ = blocks.shape
    per_angle = tile_rows // n_angle
    f32, bf16, i32 = jnp.float32, jnp.bfloat16, jnp.int32
    room = entries // 2 + per_angle + UNROLL
    params = pltpu.CompilerParams(vmem_limit_bytes=VMEM_LIMIT)
    angle = lax.axis_index("angle").astype(i32)

    partial_value, held, back_first, back_second, back_count = pl.pallas_call(
        functools.partial(forward_kernel, per_angle),
        out_shape=(
            jax.ShapeDtypeStruct((slot_count, slices, rays), bf16),
            pltpu.VMEM((entries + 1, rays, pixels), bf16),
            jax.ShapeDtypeStruct((n_angle * room,), i32),
            jax.ShapeDtypeStruct((n_angle * room,), i32),
            jax.ShapeDtypeStruct((n_angle,), i32),
        ),
        in_specs=[SMEM_SPEC, SMEM_SPEC, SMEM_SPEC, VMEM_SPEC, pl.BlockSpec(memory_space=pltpu.HBM)],
        out_specs=(VMEM_SPEC, VMEM_SPEC, SMEM_SPEC, SMEM_SPEC, SMEM_SPEC),
        scratch_shapes=[
            pltpu.VMEM((tile_rows, slices, pixels), bf16),
            pltpu.VMEM((slot_count, slices, rays), f32),
            pltpu.SMEM((entries // 2 + slot_count + UNROLL,), i32),
            pltpu.SMEM((entries // 2 + slot_count + UNROLL,), i32),
            pltpu.SMEM((slot_count,), i32),
            pltpu.SMEM((tile_rows,), i32),
            pltpu.SemaphoreType.DMA((CHUNKS,)),
        ],
        compiler_params=params,
        name="forward",
    )(tile_of, slot_of, live_count, volume, blocks)

    received = lax.all_to_all(
        partial_value.reshape((n_region, capacity, slices, rays)), "region", split_axis=0, concat_axis=0, tiled=True
    ).reshape(slot_count, slices, rays)

    residual, outgoing = pl.pallas_call(
        residual_kernel,
        out_shape=(
            jax.ShapeDtypeStruct((ray_rows, slices, rays), f32),
            jax.ShapeDtypeStruct((slot_count, slices, rays), bf16),
        ),
        in_specs=[SMEM_SPEC, VMEM_SPEC, VMEM_SPEC, VMEM_SPEC],
        out_specs=(VMEM_SPEC, VMEM_SPEC),
        scratch_shapes=[pltpu.VMEM((ray_rows, slices, rays), f32)],
        compiler_params=params,
        name="residual",
    )(ray_of, received, sinogram, ray_weight)

    returned = lax.all_to_all(
        outgoing.reshape((n_region, capacity, slices, rays)), "region", split_axis=0, concat_axis=0, tiled=True
    ).reshape(slot_count, slices, rays)

    core = (angle.reshape(1), tile_of, slot_of, back_first, back_second, back_count, held, returned)
    core_specs = [SMEM_SPEC] * 6 + [VMEM_SPEC] * 2
    first_tile = angle * per_angle
    volume_part = lax.dynamic_slice_in_dim(volume, first_tile, per_angle, 0)
    weight_part = lax.dynamic_slice_in_dim(pixel_weight, first_tile, per_angle, 0)
    scratch = [pltpu.VMEM((per_angle, slices, pixels), f32)]
    inbox = {m: [] for m in range(n_angle)}
    for mask in range(n_angle - 1, 0, -1):
        recv = inbox[mask]
        share = pl.pallas_call(
            functools.partial(backward_kernel, mask, per_angle, len(recv)),
            out_shape=jax.ShapeDtypeStruct((per_angle, slices, pixels), bf16),
            in_specs=core_specs + [VMEM_SPEC] * len(recv),
            out_specs=VMEM_SPEC,
            scratch_shapes=scratch,
            compiler_params=params,
            name=f"backward_{mask}",
        )(*core, *recv)
        hop = mask & -mask
        inbox[mask ^ hop].append(lax.ppermute(share, "angle", [(j, j ^ hop) for j in range(n_angle)]))
    recv = inbox[0]
    updated = pl.pallas_call(
        functools.partial(update_kernel, 0, per_angle, len(recv)),
        out_shape=jax.ShapeDtypeStruct((per_angle, slices, pixels), f32),
        in_specs=core_specs + [VMEM_SPEC] * (len(recv) + 2),
        out_specs=VMEM_SPEC,
        scratch_shapes=scratch,
        compiler_params=params,
        name="update",
    )(*core, *recv, volume_part, weight_part)
    return (updated, residual)


def solution(mesh):
    placed = (
        P("region", None, None),
        P(("region", "angle"), None, None),
        P(("region", "angle")),
        P(("region", "angle")),
        P(("region", "angle")),
        P(("region", "angle")),
        P(("region", "angle"), None, None),
        P(("region", "angle"), None),
        P("region", None),
    )
    return jax.shard_map(
        body,
        mesh=mesh,
        in_specs=placed,
        out_specs=(P(("region", "angle"), None, None), P(("region", "angle"), None, None)),
        check_vma=False,
    )
```

time: 210 us -> 69.2 us (0.33)
  other arithmetic: 72 us -> 0 us
  waiting for transfers between devices: 58.6 us -> 10.8 us
  matrix products: 31.2 us -> 0 us
  Pallas kernels: 0 us -> 20 us
  blocking collectives: 0 us -> 15.6 us
  between operations: 14.8 us -> 1.43 us
  local copies, waits for them, and re-layouts: 20.5 us -> 13.6 us
  starting transfers between devices: 11.1 us -> 6.9 us
    scatter-add x3 -> x0, other arithmetic: 67.3 us -> none  [the longest x1 33.2 us: body(): jax.ops.segment_sum(backward, tile_ids, num_segments=tile_rows + 1)]
    psum x1 -> x0, waiting for transfers between devices: 35.2 us -> none  [body(): all_tiles = lax.psum(gradient, 'angle')]
    dot_general x2 -> x0, matrix products: 31.2 us -> none  [the longest x1 17.4 us: body(): jnp.einsum('esp,erp->esr', picked, blocks, preferred_element_type=jnp.flo...]
    pallas_call x0 -> x6, Pallas kernels: none -> 20 us  [the longest x1 9.12 us: body(): pl.pallas_call(functools.partial(forward_kernel, per_angle), out_shape=(j...]
    gather x3 -> x0, local copies, waits for them, and re-layouts: 18.4 us -> none  [the longest x1 8.57 us: body(): picked = volume_b[tile_of]]
    all_to_all x0 -> x1, blocking collectives: none -> 15.6 us  [body(): lax.all_to_all(partial_value.reshape((n_region, capacity, slices, rays)),...]
    all_to_all x2 -> x1, waiting for transfers between devices: 23.3 us -> 8.15 us  [body(): lax.all_to_all(outgoing.reshape((n_region, capacity, slices, rays)), 'reg...]
    unnamed x8 -> x24, local copies, waits for them, and re-layouts: 0.03 us -> 12.6 us
  transfers between devices with their start and end apart: 3 -> 4, of which waited for: 3 -> 2; matrix products, arithmetic and copies ran while one was open for 0% -> 1% of each run, Pallas kernels for 0% -> 6%
where the time goes in v1:
time: 69.2 us; the launch traced here: 68.4 us
  Pallas kernels  20 us (29%)
  blocking collectives  15.6 us (23%)
  local copies, waits for them, and re-layouts  13.6 us (20%)
  waiting for transfers between devices  10.8 us (16%)
  starting transfers between devices  6.9 us (10%)
  between operations  1.43 us (2%)
    all_to_all x1, blocking collectives, body(): lax.all_to_all(partial_value.reshape((n_region, capacity, slices, rays)),...  15.6 us
    unnamed x24, local copies, waits for them, and re-layouts  12.6 us
    pallas_call x1, Pallas kernels, body(): pl.pallas_call(functools.partial(forward_kernel, per_angle), out_shape=(j...  9.12 us
    all_to_all x1, waiting for transfers between devices, body(): lax.all_to_all(outgoing.reshape((n_region, capacity, slices, rays)), 'reg...  8.15 us
    pallas_call x3, Pallas kernels, body(): pl.pallas_call(functools.partial(backward_kernel, mask, per_angle, len(re...  6.41 us
    ppermute x3, starting transfers between devices, body(): lax.ppermute(share, 'angle', [(j, j ^ hop) for j in range(n_angle)])  3.49 us
    all_to_all x1, starting transfers between devices, body(): lax.all_to_all(outgoing.reshape((n_region, capacity, slices, rays)), 'reg...  3.41 us
    pallas_call x1, Pallas kernels, body(): pl.pallas_call(functools.partial(update_kernel, 0, per_angle, len(recv)),...  2.91 us
  transfers between devices with their start and end apart: 4, of which 2 were waited for; matrix products, arithmetic and copies ran while one was open for 1% of the time, Pallas kernels for 6%

profile of v1, /device:TPU:0, one launch (start us, length us, event | category | flops | bytes accessed | tf_op | source)
XLA Modules:
  0.0 68.4 jit_solution(14025964728163706458)
XLA Ops:
  0.6 0.0 copy-start
  1.3 0.0 copy-start.4
  1.4 1.2 %copy-done.4 = f32[16,128,128]{2,1,0:T(8,128)S(1)} copy-done((f32[16,128,128]{2,1,0:T(8,128)S(1)}, f32[16,128,128]{2,1,0:T(8,128)}, u32[]{:S(2)}) %copy-start.4) | copy-done | bytes 1048600
  2.6 0.7 copy-done.6
  3.2 0.7 copy-done.8
  3.9 9.1 %forward.1 = (bf16[8,128,128]{2,1,0:T(8,128)(2,1)S(1)}, bf16[257,128,128]{2,1,0:T(8,128)(2,1)S(1)}, s32[560]{0:T(1024)S(1)}, s32[560]{0:T(1024)S(1)}, s32[4]{0:T(128)S(1)}) custom-call(s32[256]{0:T(256)S(1)} %copy-done.6, s32[256]{0:T(256)S(1)} %copy-done.8, s32[1]{0:T(128)S(6)} %copy.13.live_count, f32[16,128,128]{2,1,0:T(8,128)S(1)} %copy-done.4, ...), custom_call_target="tpu_custom_call" | custom-call | tf_op jit(solution)/shard_map/forward/pallas_call | solution.py:174
  13.1 3.2 %copy-done.1 = bf16[257,128,128]{2,1,0:T(8,128)(2,1)} copy-done((bf16[257,128,128]{2,1,0:T(8,128)(2,1)}, bf16[257,128,128]{2,1,0:T(8,128)(2,1)S(1)}, u32[]{:S(2)}) %copy-start.1) | copy-done | bytes 8421400
  16.3 15.6 %all_to_all.10 = bf16[8,1,128,128]{3,2,1,0:T(8,128)(2,1)S(1)} all-to-all(bf16[8,1,128,128]{3,2,1,0:T(8,128)(2,1)S(1)} %bitcast.14), channel_id=1, replica_groups=mesh['region'=8,'angle'=4] {'region'}, dimensions={0} | all-to-all | bytes 524288 | tf_op jit(solution)/shard_map/all_to_all | solution.py:198
  31.9 1.6 %residual.1 = (f32[8,128,128]{2,1,0:T(8,128)}, bf16[8,128,128]{2,1,0:T(8,128)(2,1)}) custom-call(s32[8]{0:T(128)S(1)} %copy-done.11, bf16[8,128,128]{2,1,0:T(8,128)(2,1)S(1)} %bitcast.13, f32[8,128,128]{2,1,0:T(8,128)S(1)} %copy-done.5, f32[8,128]{1,0:T(8,128)S(1)} %copy-done.10), custom_call_target="tpu_custom_call" | custom-call | tf_op jit(solution)/shard_map/residual/pallas_call | solution.py:202
  33.5 3.4 %all-to-all-start.1 = ((bf16[8,1,128,128]{3,2,1,0:T(8,128)(2,1)}), bf16[8,1,128,128]{3,2,1,0:T(8,128)(2,1)S(1)}, u32[]{:S(2)}, u32[]{:S(2)}) async-start(bf16[8,1,128,128]{3,2,1,0:T(8,128)(2,1)} %bitcast.5), calls=%async_computation.1 | async-start | bytes 524288 | tf_op jit(solution)/shard_map/all_to_all | solution.py:215
  36.9 8.2 %all-to-all-done.1 = bf16[8,1,128,128]{3,2,1,0:T(8,128)(2,1)S(1)} async-done(((bf16[8,1,128,128]{3,2,1,0:T(8,128)(2,1)}), bf16[8,1,128,128]{3,2,1,0:T(8,128)(2,1)S(1)}, u32[]{:S(2)}, u32[]{:S(2)}) %all-to-all-start.1) | async-done | bytes 262176 | tf_op jit(solution)/shard_map/all_to_all | solution.py:215
  45.1 3.4 %copy-done.2 = bf16[257,128,128]{2,1,0:T(8,128)(2,1)S(1)} copy-done((bf16[257,128,128]{2,1,0:T(8,128)(2,1)S(1)}, bf16[257,128,128]{2,1,0:T(8,128)(2,1)}, u32[]{:S(2)}) %copy-start.2) | copy-done | bytes 8421400
  48.5 2.1 %backward_3.1 = bf16[4,128,128]{2,1,0:T(8,128)(2,1)S(1)} custom-call(s32[1]{0:T(128)} %bitcast.refs_0_, s32[256]{0:T(256)S(1)} %copy-done.7, s32[256]{0:T(256)S(1)} %copy-done.9, s32[560]{0:T(1024)S(1)} %get-tuple-element.9.refs_3_, s32[560]{0:T(1024)S(1)} %get-tuple-element.10.refs_4_, s32[4]{0:T(128)S(1)} %get-tuple-element.11.refs_5_, ...), custom_call_target="tpu_custom_call" | custom-call | tf_op jit(solution)/shard_map/backward_3/pallas_call | solution.py:228
  50.6 0.1 collective-permute-start
  50.7 3.4 %copy-done.3 = bf16[257,128,128]{2,1,0:T(8,128)(2,1)S(1)} copy-done((bf16[257,128,128]{2,1,0:T(8,128)(2,1)S(1)}, bf16[257,128,128]{2,1,0:T(8,128)(2,1)}, u32[]{:S(2)}) %copy-start.3) | copy-done | bytes 8421400
  54.1 2.1 %backward_1.1 = bf16[4,128,128]{2,1,0:T(8,128)(2,1)S(1)} custom-call(s32[1]{0:T(128)} %bitcast.refs_0_, s32[256]{0:T(256)S(1)} %copy-done.7, s32[256]{0:T(256)S(1)} %copy-done.9, s32[560]{0:T(1024)S(1)} %get-tuple-element.9.refs_3_, s32[560]{0:T(1024)S(1)} %get-tuple-element.10.refs_4_, s32[4]{0:T(128)S(1)} %get-tuple-element.11.refs_5_, ...), custom_call_target="tpu_custom_call" | custom-call | tf_op jit(solution)/shard_map/backward_1/pallas_call | solution.py:228
  56.2 0.6 collective-permute-start.2
  56.8 0.0 collective-permute-done.refs_8_
  56.8 2.1 %backward_2.1 = bf16[4,128,128]{2,1,0:T(8,128)(2,1)S(1)} custom-call(s32[1]{0:T(128)} %bitcast.refs_0_, s32[256]{0:T(256)S(1)} %copy-done.7, s32[256]{0:T(256)S(1)} %copy-done.9, s32[560]{0:T(1024)S(1)} %get-tuple-element.9.refs_3_, s32[560]{0:T(1024)S(1)} %get-tuple-element.10.refs_4_, s32[4]{0:T(128)S(1)} %get-tuple-element.11.refs_5_, ...), custom_call_target="tpu_custom_call" | custom-call | tf_op jit(solution)/shard_map/backward_2/pallas_call | solution.py:228
  59.0 2.8 %collective-permute-start.1 = (bf16[4,128,128]{2,1,0:T(8,128)(2,1)S(1)}, bf16[4,128,128]{2,1,0:T(8,128)(2,1)S(1)}, u32[]{:S(2)}, u32[]{:S(2)}) collective-permute-start(bf16[4,128,128]{2,1,0:T(8,128)(2,1)S(1)} %backward_2.1), channel_id=1, source_target_pairs={{0,2},{1,3},{2,0},{3,1},{4,6},{5,7},{6,4},{7,5},{8,10},{9,11},{10,... | collective-permute-start | bytes 393224 | tf_op jit(solution)/shard_map/ppermute | solution.py:238
  61.8 1.0 %constant_dynamic-slice_fusion.1.refs_10_ = f32[4,128,128]{2,1,0:T(8,128)S(1)} fusion(f32[16,128,128]{2,1,0:T(8,128)} %volume.1, s32[]{:T(128)S(6)} %select_n.4), kind=kLoop, calls=%fused_computation.1 | loop fusion | bytes 524292 | tf_op jit(solution)/shard_map/dynamic_slice | solution.py:222
  62.8 0.0 collective-permute-done.2.refs_9_
  62.8 2.7 %collective-permute-done.1.refs_8_ = bf16[4,128,128]{2,1,0:T(8,128)(2,1)S(1)} collective-permute-done((bf16[4,128,128]{2,1,0:T(8,128)(2,1)S(1)}, bf16[4,128,128]{2,1,0:T(8,128)(2,1)S(1)}, u32[]{:S(2)}, u32[]{:S(2)}) %collective-permute-start.1) | collective-permute-done | bytes 131104 | tf_op jit(solution)/shard_map/ppermute | solution.py:238
  65.5 2.9 %update.1 = f32[4,128,128]{2,1,0:T(8,128)} custom-call(s32[1]{0:T(128)} %bitcast.refs_0_, s32[256]{0:T(256)S(1)} %copy-done.7, s32[256]{0:T(256)S(1)} %copy-done.9, s32[560]{0:T(1024)S(1)} %get-tuple-element.9.refs_3_, s32[560]{0:T(1024)S(1)} %get-tuple-element.10.refs_4_, s32[4]{0:T(128)S(1)} %get-tuple-element.11.refs_5_, ...), custom_call_target="tpu_custom_call" | custom-call | tf_op jit(solution)/shard_map/update/pallas_call | solution.py:240
  (17 shorter events, 0.0 us)
Async XLA Ops:
  0.6 61.2 %copy-start = (f32[16,128]{1,0:T(8,128)S(1)}, f32[16,128]{1,0:T(8,128)}, u32[]{:S(2)}) copy-start(f32[16,128]{1,0:T(8,128)} %param.17) | copy-start | bytes 24580
  0.6 44.4 %copy-start.7 = (s32[256]{0:T(256)S(1)}, s32[256]{0:T(256)}, u32[]{:S(2)}) copy-start(s32[256]{0:T(256)} %refs_1_.7) | copy-start | bytes 3076
  0.7 31.2 %copy-start.11 = (s32[8]{0:T(128)S(1)}, s32[8]{0:T(128)}, u32[]{:S(2)}) copy-start(s32[8]{0:T(128)} %ray_of.1) | copy-start | bytes 100
  1.3 1.2 %copy-start.4 = (f32[16,128,128]{2,1,0:T(8,128)S(1)}, f32[16,128,128]{2,1,0:T(8,128)}, u32[]{:S(2)}) copy-start(f32[16,128,128]{2,1,0:T(8,128)} %volume.1) | copy-start | bytes 3145732
  2.6 0.7 copy-start.6
  3.2 0.7 copy-start.8
  3.9 28.0 %copy-start.5 = (f32[8,128,128]{2,1,0:T(8,128)S(1)}, f32[8,128,128]{2,1,0:T(8,128)}, u32[]{:S(2)}) copy-start(f32[8,128,128]{2,1,0:T(8,128)} %sinogram.1) | copy-start | bytes 1572868
  3.9 28.0 %copy-start.10 = (f32[8,128]{1,0:T(8,128)S(1)}, f32[8,128]{1,0:T(8,128)}, u32[]{:S(2)}) copy-start(f32[8,128]{1,0:T(8,128)} %ray_weight.1) | copy-start | bytes 12292
  3.9 41.2 %copy-start.9 = (s32[256]{0:T(256)S(1)}, s32[256]{0:T(256)}, u32[]{:S(2)}) copy-start(s32[256]{0:T(256)} %refs_2_.7) | copy-start | bytes 3076
  13.1 3.2 %copy-start.1 = (bf16[257,128,128]{2,1,0:T(8,128)(2,1)}, bf16[257,128,128]{2,1,0:T(8,128)(2,1)S(1)}, u32[]{:S(2)}) copy-start(bf16[257,128,128]{2,1,0:T(8,128)(2,1)S(1)} %get-tuple-element.12.refs_6_) | copy-start | bytes 25264132
  33.5 11.6 %all-to-all-start.1 = ((bf16[8,1,128,128]{3,2,1,0:T(8,128)(2,1)}), bf16[8,1,128,128]{3,2,1,0:T(8,128)(2,1)S(1)}, u32[]{:S(2)}, u32[]{:S(2)}) async-start(bf16[8,1,128,128]{3,2,1,0:T(8,128)(2,1)} %bitcast.5), calls=%async_computation.1 | async-start | bytes 524288 | tf_op jit(solution)/shard_map/all_to_all | solution.py:215
  45.1 3.4 %copy-start.2 = (bf16[257,128,128]{2,1,0:T(8,128)(2,1)S(1)}, bf16[257,128,128]{2,1,0:T(8,128)(2,1)}, u32[]{:S(2)}) copy-start(bf16[257,128,128]{2,1,0:T(8,128)(2,1)} %copy-done.1) | copy-start | bytes 25264132
  50.6 6.2 %collective-permute-start = (bf16[4,128,128]{2,1,0:T(8,128)(2,1)S(1)}, bf16[4,128,128]{2,1,0:T(8,128)(2,1)S(1)}, u32[]{:S(2)}, u32[]{:S(2)}) collective-permute-start(bf16[4,128,128]{2,1,0:T(8,128)(2,1)S(1)} %backward_3.1), channel_id=1, source_target_pairs={{0,1},{1,0},{2,3},{3,2},{4,5},{5,4},{6,7},{7,6},{8,9},{9,8},{10,11... | collective-permute-start | bytes 393224 | tf_op jit(solution)/shard_map/ppermute | solution.py:238
  50.7 3.4 %copy-start.3 = (bf16[257,128,128]{2,1,0:T(8,128)(2,1)S(1)}, bf16[257,128,128]{2,1,0:T(8,128)(2,1)}, u32[]{:S(2)}) copy-start(bf16[257,128,128]{2,1,0:T(8,128)(2,1)} %copy-done.1) | copy-start | bytes 25264132
  56.2 6.6 %collective-permute-start.2 = (bf16[4,128,128]{2,1,0:T(8,128)(2,1)S(1)}, bf16[4,128,128]{2,1,0:T(8,128)(2,1)S(1)}, u32[]{:S(2)}, u32[]{:S(2)}) collective-permute-start(bf16[4,128,128]{2,1,0:T(8,128)(2,1)S(1)} %backward_1.1), channel_id=1, source_target_pairs={{0,1},{1,0},{2,3},{3,2},{4,5},{5,4},{6,7},{7,6},{8,9},{9,8},{10,11... | collective-permute-start | bytes 393224 | tf_op jit(solution)/shard_map/ppermute | solution.py:238
  59.0 6.5 %collective-permute-start.1 = (bf16[4,128,128]{2,1,0:T(8,128)(2,1)S(1)}, bf16[4,128,128]{2,1,0:T(8,128)(2,1)S(1)}, u32[]{:S(2)}, u32[]{:S(2)}) collective-permute-start(bf16[4,128,128]{2,1,0:T(8,128)(2,1)S(1)} %backward_2.1), channel_id=1, source_target_pairs={{0,2},{1,3},{2,0},{3,1},{4,6},{5,7},{6,4},{7,5},{8,10},{9,11},{10,... | collective-permute-start | bytes 393224 | tf_op jit(solution)/shard_map/ppermute | solution.py:238

commit v2 on v0

v2 whole, which is shorter than its diff:
```python
import functools

import jax
import jax.numpy as jnp
from jax import lax
from jax.experimental import pallas as pl
from jax.experimental.pallas import tpu as pltpu
from jax.sharding import PartitionSpec as P

FORWARD_UNROLL = 64
BACKWARD_UNROLL = 16
CHUNKS = 8
SLOT_BIT = 1 << 16
TILE_BIT = 1 << 24
VMEM_LIMIT = 24 * 1024 * 1024
SMEM_SPEC = pl.BlockSpec(memory_space=pltpu.SMEM)
VMEM_SPEC = pl.BlockSpec(memory_space=pltpu.VMEM)
MAYBE_HBM = jax.ShapeDtypeStruct
HBM_SPEC = pl.BlockSpec(memory_space=pltpu.HBM)


def dot(x, y):
    return lax.dot_general(x, y, (((1,), (0,)), ((), ())), preferred_element_type=jnp.float32)


def ceil_div(a, b):
    return lax.div(a + (b - 1), jnp.int32(b))


def split_tile(tile, per_angle):
    if per_angle & (per_angle - 1) == 0:
        return lax.shift_right_logical(tile, per_angle.bit_length() - 1), jnp.bitwise_and(tile, per_angle - 1)
    return lax.div(tile, jnp.int32(per_angle)), lax.rem(tile, jnp.int32(per_angle))


def away(group, me, groups):
    if groups & (groups - 1) == 0:
        return jnp.bitwise_xor(group, me)
    return lax.rem(group - me + groups, jnp.int32(groups))


def forward_kernel(per_angle, groups, room, unroll, live_count, tile_hbm, slot_hbm, volume_hbm, blocks_hbm,
                   partial_out, lists, kept, tile_of, slot_of, volume, volume_b, total, held, sems, block_sems, kept_sem):
    entries = blocks_hbm.shape[0]
    slot_count, tile_rows = partial_out.shape[0], volume.shape[0]
    chunks = block_sems.shape[0]
    chunk = entries // chunks

    def block_copy(c):
        part = pl.ds(c * chunk, chunk)
        return pltpu.make_async_copy(blocks_hbm.at[part], held.at[part], block_sems.at[c])

    small = [
        pltpu.make_async_copy(slot_hbm, slot_of, sems.at[0]),
        pltpu.make_async_copy(tile_hbm, tile_of, sems.at[1]),
        pltpu.make_async_copy(volume_hbm, volume, sems.at[2]),
    ]
    for copy in small:
        copy.start()
    for c in range(chunks):
        block_copy(c).start()
    keep = pltpu.make_async_copy(blocks_hbm, kept, kept_sem)
    keep.start()
    me = lax.axis_index("angle").astype(jnp.int32)
    total[...] = jnp.zeros_like(total)
    for g in range(groups):
        lists[g] = 0
    for copy in small:
        copy.wait()
    live = live_count[0]
    for t in range(tile_rows):
        volume_b[t] = volume[t].T.astype(jnp.bfloat16)

    def step(i, _):
        for u in range(unroll):
            e = i * unroll + u
            if u % chunk == 0:
                block_copy(lax.div(e, jnp.int32(chunk))).wait()
            is_live = e < live
            s, t = slot_of[e], tile_of[e]
            total[jnp.where(is_live, s, slot_count)] += dot(held[e], volume_b[t])
            g, row = split_tile(t, per_angle)
            g = away(g, me, groups)
            m = lists[g]
            lists[groups + g * room + m] = e + s * SLOT_BIT + row * TILE_BIT
            lists[g] = m + is_live.astype(jnp.int32)
        return 0

    steps = ceil_div(live, unroll)
    lax.fori_loop(0, steps, step, 0)
    for g in range(groups):
        m = lists[g]
        for u in range(BACKWARD_UNROLL):
            lists[groups + g * room + m + u] = per_angle * TILE_BIT
    for s in range(slot_count):
        partial_out[s] = total[s].T.astype(partial_out.dtype)
    per_step = unroll // chunk
    lax.fori_loop(steps * per_step, chunks, lambda c, _: (block_copy(c).wait(), 0)[1], 0)
    keep.wait()


def residual_kernel(ray_of, received, sinogram, ray_weight, residual, outgoing, total):
    total[...] = jnp.zeros_like(total)
    slot_count, ray_rows = received.shape[0], sinogram.shape[0]
    for r in range(slot_count):
        total[ray_of[r]] += received[r].astype(jnp.float32)
    residual[...] = ray_weight[...][:, None, :] * (sinogram[...] - total[...])
    for r in range(slot_count):
        outgoing[r] = residual[ray_of[r]].astype(outgoing.dtype)


def backward_sums(mask, groups, per_angle, lists, held, returned, total):
    room = (lists.shape[0] - groups) // groups
    total[...] = jnp.zeros_like(total)
    first = groups + mask * room

    def multiply(i, _):
        for u in range(BACKWARD_UNROLL):
            word = lists[first + i * BACKWARD_UNROLL + u]
            e = jnp.bitwise_and(word, SLOT_BIT - 1)
            s = jnp.bitwise_and(lax.shift_right_logical(word, 16), 255)
            total[lax.shift_right_logical(word, 24)] += dot(returned[s], held[e])
        return 0

    lax.fori_loop(0, ceil_div(lists[mask], BACKWARD_UNROLL), multiply, 0)
    return total[pl.ds(0, per_angle)]


def backward_kernel(mask, groups, n_recv, lists, held, returned, *refs):
    recv, (out, total) = refs[:n_recv], refs[n_recv:]
    value = backward_sums(mask, groups, out.shape[0], lists, held, returned, total)
    for piece in recv:
        value = value + piece[...].astype(jnp.float32)
    out[...] = value.astype(out.dtype)


def own_kernel(groups, lists, held, returned, volume_hbm, weight_hbm, out, weight_out, volume, weight, total, sems):
    per_angle = out.shape[0]
    mine = pl.ds(lax.axis_index("angle").astype(jnp.int32) * per_angle, per_angle)
    copies = [
        pltpu.make_async_copy(volume_hbm.at[mine], volume, sems.at[0]),
        pltpu.make_async_copy(weight_hbm, weight, sems.at[1]),
    ]
    for copy in copies:
        copy.start()
    value = backward_sums(0, groups, per_angle, lists, held, returned, total)
    for copy in copies:
        copy.wait()
    rows = weight[mine][:, None, :]
    weight_out[...] = rows
    out[...] = volume[...] + rows * value


def update_kernel(n_recv, own, weight, *refs):
    recv, out = refs[:n_recv], refs[n_recv]
    value = recv[0][...].astype(jnp.float32)
    for piece in recv[1:]:
        value = value + piece[...].astype(jnp.float32)
    out[...] = own[...] + weight[...] * value


def body(volume, blocks, tile_of, slot_of, live_count, ray_of, sinogram, ray_weight, pixel_weight):
    n_region = lax.axis_size("region")
    n_angle = lax.axis_size("angle")
    slot_count = ray_of.shape[0]
    capacity = slot_count // n_region
    ray_rows = sinogram.shape[0]
    tile_rows, slices, pixels = volume.shape
    entries, rays, _ = blocks.shape
    per_angle = tile_rows // n_angle
    f32, bf16, i32 = jnp.float32, jnp.bfloat16, jnp.int32
    room = entries + BACKWARD_UNROLL
    unroll = min(FORWARD_UNROLL, entries)
    chunks = min(CHUNKS, entries)
    params = pltpu.CompilerParams(vmem_limit_bytes=VMEM_LIMIT)
    in_hbm = functools.partial(pltpu.with_memory_space_constraint, memory_space=pltpu.HBM)
    in_vmem = functools.partial(pltpu.with_memory_space_constraint, memory_space=pltpu.VMEM)
    list_size = n_angle * (room + 1)

    partial_value, lists, kept = pl.pallas_call(
        functools.partial(forward_kernel, per_angle, n_angle, room, unroll),
        out_shape=(
            MAYBE_HBM((slot_count, slices, rays), bf16),
            jax.ShapeDtypeStruct((list_size,), i32),
            pltpu.VMEM(blocks.shape, bf16),
        ),
        in_specs=[SMEM_SPEC] + [HBM_SPEC] * 4,
        out_specs=(VMEM_SPEC, SMEM_SPEC, pl.BlockSpec(memory_space=pl.ANY)),
        scratch_shapes=[
            pltpu.SMEM((entries,), i32),
            pltpu.SMEM((entries,), i32),
            pltpu.VMEM((tile_rows, slices, pixels), f32),
            pltpu.VMEM((tile_rows, slices, pixels), bf16),
            pltpu.VMEM((slot_count + 1, slices, rays), f32),
            pltpu.VMEM((entries, rays, pixels), bf16),
            pltpu.SemaphoreType.DMA((3,)),
            pltpu.SemaphoreType.DMA((chunks,)),
            pltpu.SemaphoreType.DMA,
        ],
        compiler_params=params,
        name="forward",
    )(live_count, *[in_hbm(x) for x in (tile_of, slot_of, volume, blocks)])

    received = lax.all_to_all(
        partial_value.reshape((n_region, capacity, slices, rays)), "region", split_axis=0, concat_axis=0, tiled=True
    ).reshape(slot_count, slices, rays)

    residual, outgoing = pl.pallas_call(
        residual_kernel,
        out_shape=(
            jax.ShapeDtypeStruct((ray_rows, slices, rays), f32),
            MAYBE_HBM((slot_count, slices, rays), bf16),
        ),
        in_specs=[SMEM_SPEC, VMEM_SPEC, VMEM_SPEC, VMEM_SPEC],
        out_specs=(VMEM_SPEC, VMEM_SPEC),
        scratch_shapes=[pltpu.VMEM((ray_rows, slices, rays), f32)],
        compiler_params=params,
        name="residual",
    )(ray_of, received, sinogram, ray_weight)

    returned = lax.all_to_all(
        outgoing.reshape((n_region, capacity, slices, rays)), "region", split_axis=0, concat_axis=0, tiled=True
    ).reshape(slot_count, slices, rays)

    held_in = kept
    held_in = in_vmem(held_in)

    def backward(mask, recv):
        return pl.pallas_call(
            functools.partial(backward_kernel, mask, n_angle, len(recv)),
            out_shape=jax.ShapeDtypeStruct((per_angle, slices, pixels), bf16),
            in_specs=[SMEM_SPEC] + [VMEM_SPEC] * (2 + len(recv)),
            out_specs=VMEM_SPEC,
            scratch_shapes=[pltpu.VMEM((per_angle + 1, slices, pixels), f32)],
            compiler_params=params,
            name=f"backward_{mask}",
        )(lists, held_in, returned, *recv)

    paired = n_angle & (n_angle - 1) == 0
    inbox = {m: [] for m in range(n_angle)}
    for mask in range(n_angle - 1, 0, -1):
        share = backward(mask, inbox[mask])
        if paired:
            hop = mask & -mask
            there = [(j, j ^ hop) for j in range(n_angle)]
            inbox[mask ^ hop].append(lax.ppermute(share, "angle", there))
        else:
            there = [(j, (j + mask) % n_angle) for j in range(n_angle)]
            inbox[0].append(lax.ppermute(share, "angle", there))
    own, weight = pl.pallas_call(
        functools.partial(own_kernel, n_angle),
        out_shape=(
            jax.ShapeDtypeStruct((per_angle, slices, pixels), f32),
            jax.ShapeDtypeStruct((per_angle, 1, pixels), f32),
        ),
        in_specs=[SMEM_SPEC] + [VMEM_SPEC] * 2 + [HBM_SPEC] * 2,
        out_specs=(VMEM_SPEC, VMEM_SPEC),
        scratch_shapes=[
            pltpu.VMEM((per_angle, slices, pixels), f32),
            pltpu.VMEM(pixel_weight.shape, f32),
            pltpu.VMEM((per_angle + 1, slices, pixels), f32),
            pltpu.SemaphoreType.DMA((2,)),
        ],
        compiler_params=params,
        name="own",
    )(lists, held_in, returned, in_hbm(volume), in_hbm(pixel_weight))
    recv = inbox[0]
    updated = pl.pallas_call(
        functools.partial(update_kernel, len(recv)),
        out_shape=jax.ShapeDtypeStruct((per_angle, slices, pixels), f32),
        in_specs=[VMEM_SPEC] * (len(recv) + 2),
        out_specs=VMEM_SPEC,
        compiler_params=params,
        name="update",
    )(own, weight, *recv)
    return (updated, residual)


def solution(mesh):
    placed = (
        P("region", None, None),
        P(("region", "angle"), None, None),
        P(("region", "angle")),
        P(("region", "angle")),
        P(("region", "angle")),
        P(("region", "angle")),
        P(("region", "angle"), None, None),
        P(("region", "angle"), None),
        P("region", None),
    )
    return jax.shard_map(
        body,
        mesh=mesh,
        in_specs=placed,
        out_specs=(P(("region", "angle"), None, None), P(("region", "angle"), None, None)),
        check_vma=False,
    )
```

time: 210 us -> 50.4 us (0.24)
  other arithmetic: 72 us -> 0 us
  waiting for transfers between devices: 58.6 us -> 2.93 us
  matrix products: 31.2 us -> 0 us
  blocking collectives: 0 us -> 27 us
  local copies, waits for them, and re-layouts: 20.5 us -> 0.01 us
  Pallas kernels: 0 us -> 18 us
  between operations: 14.8 us -> 1.42 us
  starting transfers between devices: 11.1 us -> 1.23 us
    scatter-add x3 -> x0, other arithmetic: 67.3 us -> none  [the longest x1 33.2 us: body(): jax.ops.segment_sum(backward, tile_ids, num_segments=tile_rows + 1)]
    psum x1 -> x0, waiting for transfers between devices: 35.2 us -> none  [body(): all_tiles = lax.psum(gradient, 'angle')]
    dot_general x2 -> x0, matrix products: 31.2 us -> none  [the longest x1 17.4 us: body(): jnp.einsum('esp,erp->esr', picked, blocks, preferred_element_type=jnp.flo...]
    all_to_all x0 -> x2, blocking collectives: none -> 27 us  [the longest x1 15.1 us: body(): lax.all_to_all(partial_value.reshape((n_region, capacity, slices, rays)),...]
    all_to_all x2 -> x0, waiting for transfers between devices: 23.3 us -> none  [the longest x1 14.5 us: body(): lax.all_to_all(partial_value.reshape((n_region, capacity) + partial_value...]
    gather x3 -> x0, local copies, waits for them, and re-layouts: 18.4 us -> none  [the longest x1 8.57 us: body(): picked = volume_b[tile_of]]
    pallas_call x0 -> x7, Pallas kernels: none -> 18 us  [the longest x1 8.37 us: body(): pl.pallas_call(functools.partial(forward_kernel, per_angle, n_angle, room...]
    all_to_all x2 -> x0, starting transfers between devices: 10.9 us -> none  [the longest x1 7.28 us: body(): lax.all_to_all(partial_value.reshape((n_region, capacity) + partial_value...]
  transfers between devices with their start and end apart: 3 -> 3, of which waited for: 3 -> 1; matrix products, arithmetic and copies ran while one was open for 0% -> 0% of each run, Pallas kernels for 0% -> 11%
where the time goes in v2:
time: 50.4 us; the launch traced here: 50.6 us
  blocking collectives  27 us (54%)
  Pallas kernels  18 us (36%)
  waiting for transfers between devices  2.93 us (6%)
  between operations  1.42 us (3%)
  starting transfers between devices  1.23 us (2%)
    all_to_all x1, blocking collectives, body(): lax.all_to_all(partial_value.reshape((n_region, capacity, slices, rays)),...  15.1 us
    all_to_all x1, blocking collectives, body(): lax.all_to_all(outgoing.reshape((n_region, capacity, slices, rays)), 'reg...  11.9 us
    pallas_call x1, Pallas kernels, body(): pl.pallas_call(functools.partial(forward_kernel, per_angle, n_angle, room...  8.37 us
    pallas_call x3, Pallas kernels, backward(): pl.pallas_call(functools.partial(backward_kernel, mask, n_angle, len(recv...  5.41 us
    ppermute x3, waiting for transfers between devices, body(): inbox[mask ^ hop].append(lax.ppermute(share, 'angle', there))  2.93 us
    pallas_call x1, Pallas kernels, body(): pl.pallas_call(functools.partial(own_kernel, n_angle), out_shape=(jax.Sha...  1.94 us
    pallas_call x1, Pallas kernels, body(): pl.pallas_call(residual_kernel, out_shape=(jax.ShapeDtypeStruct((ray_rows...  1.52 us
    ppermute x3, starting transfers between devices, body(): inbox[mask ^ hop].append(lax.ppermute(share, 'angle', there))  1.23 us
  transfers between devices with their start and end apart: 3, of which 1 were waited for; matrix products, arithmetic and copies ran while one was open for 0% of the time, Pallas kernels for 11%

profile of v2, /device:TPU:0, one launch (start us, length us, event | category | flops | bytes accessed | tf_op | source)
XLA Modules:
  0.0 50.6 jit_solution(2986865762972397756)
XLA Ops:
  0.6 0.0 copy-start.1
  0.6 0.0 copy-start
  0.7 0.0 copy-start.2
  1.4 8.4 %forward.1 = (bf16[8,128,128]{2,1,0:T(8,128)(2,1)S(1)}, s32[1092]{0:T(1024)S(1)}, bf16[256,128,128]{2,1,0:T(8,128)(2,1)S(1)}) custom-call(s32[1]{0:T(128)S(6)} %copy.13.live_count, s32[256]{0:T(256)} %tile_hbm.1, s32[256]{0:T(256)} %slot_hbm.1, f32[16,128,128]{2,1,0:T(8,128)} %volume_hbm.3, bf16[256,128,128]{2,1,0:T(8,128)(2,1)} %blocks_hbm.1), custom_call_target="tpu_custom_call" | custom-call | tf_op jit(solution)/shard_map/forward/pallas_call | solution.py:180
  9.7 15.1 %all_to_all.10 = bf16[8,1,128,128]{3,2,1,0:T(8,128)(2,1)S(1)} all-to-all(bf16[8,1,128,128]{3,2,1,0:T(8,128)(2,1)S(1)} %bitcast.13), channel_id=1, replica_groups=mesh['region'=8,'angle'=4] {'region'}, dimensions={0} | all-to-all | bytes 524288 | tf_op jit(solution)/shard_map/all_to_all | solution.py:204
  24.8 0.0 copy-done.1
  24.8 0.0 copy-done
  24.8 0.0 copy-done.2
  24.8 1.5 %residual.1 = (f32[8,128,128]{2,1,0:T(8,128)}, bf16[8,128,128]{2,1,0:T(8,128)(2,1)S(1)}) custom-call(s32[8]{0:T(128)S(1)} %copy-done.2, bf16[8,128,128]{2,1,0:T(8,128)(2,1)S(1)} %bitcast.12, f32[8,128,128]{2,1,0:T(8,128)S(1)} %copy-done, f32[8,128]{1,0:T(8,128)S(1)} %copy-done.1), custom_call_target="tpu_custom_call" | custom-call | tf_op jit(solution)/shard_map/residual/pallas_call | solution.py:208
  26.3 11.9 %all_to_all.11 = bf16[8,1,128,128]{3,2,1,0:T(8,128)(2,1)S(1)} all-to-all(bf16[8,1,128,128]{3,2,1,0:T(8,128)(2,1)S(1)} %bitcast.14), channel_id=1, replica_groups=mesh['region'=8,'angle'=4] {'region'}, dimensions={0} | all-to-all | bytes 524288 | tf_op jit(solution)/shard_map/all_to_all | solution.py:221
  38.3 1.9 %backward_3.1 = bf16[4,128,128]{2,1,0:T(8,128)(2,1)S(1)} custom-call(s32[1092]{0:T(1024)S(1)} %get-tuple-element.9.lists, bf16[256,128,128]{2,1,0:T(8,128)(2,1)S(1)} %get-tuple-element.10.held, bf16[8,128,128]{2,1,0:T(8,128)(2,1)S(1)} %bitcast.8), custom_call_target="tpu_custom_call" | custom-call | tf_op jit(solution)/shard_map/backward_3/pallas_call | solution.py:229
  40.2 0.1 collective-permute-start
  40.3 1.6 %backward_1.1 = bf16[4,128,128]{2,1,0:T(8,128)(2,1)S(1)} custom-call(s32[1092]{0:T(1024)S(1)} %get-tuple-element.9.lists, bf16[256,128,128]{2,1,0:T(8,128)(2,1)S(1)} %get-tuple-element.10.held, bf16[8,128,128]{2,1,0:T(8,128)(2,1)S(1)} %bitcast.9), custom_call_target="tpu_custom_call" | custom-call | tf_op jit(solution)/shard_map/backward_1/pallas_call | solution.py:229
  41.9 0.9 %collective-permute-start.2 = (bf16[4,128,128]{2,1,0:T(8,128)(2,1)S(1)}, bf16[4,128,128]{2,1,0:T(8,128)(2,1)S(1)}, u32[]{:S(2)}, u32[]{:S(2)}) collective-permute-start(bf16[4,128,128]{2,1,0:T(8,128)(2,1)S(1)} %backward_1.1), channel_id=1, source_target_pairs={{0,1},{1,0},{2,3},{3,2},{4,5},{5,4},{6,7},{7,6},{8,9},{9,8},{10,11... | collective-permute-start | bytes 393224 | tf_op jit(solution)/shard_map/ppermute | solution.py:246
  42.7 0.0 collective-permute-done.refs_0_
  42.7 1.9 %backward_2.1 = bf16[4,128,128]{2,1,0:T(8,128)(2,1)S(1)} custom-call(s32[1092]{0:T(1024)S(1)} %get-tuple-element.9.lists, bf16[256,128,128]{2,1,0:T(8,128)(2,1)S(1)} %get-tuple-element.10.held, bf16[8,128,128]{2,1,0:T(8,128)(2,1)S(1)} %bitcast.10, bf16[4,128,128]{2,1,0:T(8,128)(2,1)S(1)} %collective-permute-done.refs_0_), custom_call_target="tpu_custom_call" | custom-call | tf_op jit(solution)/shard_map/backward_2/pallas_call | solution.py:229
  44.7 0.3 collective-permute-start.1
  44.9 1.9 %own.1 = (f32[4,128,128]{2,1,0:T(8,128)S(1)}, f32[4,1,128]{2,1,0:T(1,128)S(1)}) custom-call(s32[1092]{0:T(1024)S(1)} %get-tuple-element.9.lists, bf16[256,128,128]{2,1,0:T(8,128)(2,1)S(1)} %get-tuple-element.10.held, bf16[8,128,128]{2,1,0:T(8,128)(2,1)S(1)} %bitcast.11, f32[16,128,128]{2,1,0:T(8,128)} %volume_hbm.3, f32[16,128]{1,0:T(8,128)} %weight_hbm.1), custom_call_target="tpu_custom_call" | custom-call | tf_op jit(solution)/shard_map/own/pallas_call | solution.py:250
  46.9 0.0 collective-permute-done.2.refs_1_
  46.9 2.9 %collective-permute-done.1.refs_0_ = bf16[4,128,128]{2,1,0:T(8,128)(2,1)S(1)} collective-permute-done((bf16[4,128,128]{2,1,0:T(8,128)(2,1)S(1)}, bf16[4,128,128]{2,1,0:T(8,128)(2,1)S(1)}, u32[]{:S(2)}, u32[]{:S(2)}) %collective-permute-start.1) | collective-permute-done | bytes 131104 | tf_op jit(solution)/shard_map/ppermute | solution.py:246
  49.8 0.8 %update.1 = f32[4,128,128]{2,1,0:T(8,128)} custom-call(f32[4,128,128]{2,1,0:T(8,128)S(1)} %get-tuple-element.13.own, f32[4,1,128]{2,1,0:T(1,128)S(1)} %get-tuple-element.14.weight, bf16[4,128,128]{2,1,0:T(8,128)(2,1)S(1)} %collective-permute-done.1.refs_0_, bf16[4,128,128]{2,1,0:T(8,128)(2,1)S(1)} %collective-permute-done.2.refs_1_), custom_call_target="tpu_custom_call" | custom-call | tf_op jit(solution)/shard_map/update/pallas_call | solution.py:268
Async XLA Ops:
  0.6 24.2 %copy-start.1 = (f32[8,128]{1,0:T(8,128)S(1)}, f32[8,128]{1,0:T(8,128)}, u32[]{:S(2)}) copy-start(f32[8,128]{1,0:T(8,128)} %ray_weight.1) | copy-start | bytes 12292
  0.6 24.2 %copy-start = (f32[8,128,128]{2,1,0:T(8,128)S(1)}, f32[8,128,128]{2,1,0:T(8,128)}, u32[]{:S(2)}) copy-start(f32[8,128,128]{2,1,0:T(8,128)} %sinogram.1) | copy-start | bytes 1572868
  0.7 24.2 %copy-start.2 = (s32[8]{0:T(128)S(1)}, s32[8]{0:T(128)}, u32[]{:S(2)}) copy-start(s32[8]{0:T(128)} %ray_of.1) | copy-start | bytes 100
  40.2 2.6 %collective-permute-start = (bf16[4,128,128]{2,1,0:T(8,128)(2,1)S(1)}, bf16[4,128,128]{2,1,0:T(8,128)(2,1)S(1)}, u32[]{:S(2)}, u32[]{:S(2)}) collective-permute-start(bf16[4,128,128]{2,1,0:T(8,128)(2,1)S(1)} %backward_3.1), channel_id=1, source_target_pairs={{0,1},{1,0},{2,3},{3,2},{4,5},{5,4},{6,7},{7,6},{8,9},{9,8},{10,11... | collective-permute-start | bytes 393224 | tf_op jit(solution)/shard_map/ppermute | solution.py:246
  41.9 5.0 %collective-permute-start.2 = (bf16[4,128,128]{2,1,0:T(8,128)(2,1)S(1)}, bf16[4,128,128]{2,1,0:T(8,128)(2,1)S(1)}, u32[]{:S(2)}, u32[]{:S(2)}) collective-permute-start(bf16[4,128,128]{2,1,0:T(8,128)(2,1)S(1)} %backward_1.1), channel_id=1, source_target_pairs={{0,1},{1,0},{2,3},{3,2},{4,5},{5,4},{6,7},{7,6},{8,9},{9,8},{10,11... | collective-permute-start | bytes 393224 | tf_op jit(solution)/shard_map/ppermute | solution.py:246
  44.7 5.2 %collective-permute-start.1 = (bf16[4,128,128]{2,1,0:T(8,128)(2,1)S(1)}, bf16[4,128,128]{2,1,0:T(8,128)(2,1)S(1)}, u32[]{:S(2)}, u32[]{:S(2)}) collective-permute-start(bf16[4,128,128]{2,1,0:T(8,128)(2,1)S(1)} %backward_2.1), channel_id=1, source_target_pairs={{0,2},{1,3},{2,0},{3,1},{4,6},{5,7},{6,4},{7,5},{8,10},{9,11},{10,... | collective-permute-start | bytes 393224 | tf_op jit(solution)/shard_map/ppermute | solution.py:246

commit v3 on v2

v3 whole, which is shorter than its diff:
```python
import functools

import jax
import jax.numpy as jnp
from jax import lax
from jax.experimental import pallas as pl
from jax.experimental.pallas import tpu as pltpu
from jax.sharding import PartitionSpec as P

FORWARD_PARTS = 2
BACKWARD_PAIRS = 16
SLOT_BIT = 1 << 16
TILE_BIT = 1 << 24
VMEM_LIMIT = 24 * 1024 * 1024
SMEM_SPEC = pl.BlockSpec(memory_space=pltpu.SMEM)
VMEM_SPEC = pl.BlockSpec(memory_space=pltpu.VMEM)
MAYBE_HBM = jax.ShapeDtypeStruct
HBM_SPEC = pl.BlockSpec(memory_space=pltpu.HBM)


def dot(x, y):
    return lax.dot_general(x, y, (((1,), (0,)), ((), ())), preferred_element_type=jnp.float32)


def ceil_div(a, b):
    return lax.div(a + (b - 1), jnp.int32(b))


def split_tile(tile, per_angle):
    if per_angle & (per_angle - 1) == 0:
        return lax.shift_right_logical(tile, per_angle.bit_length() - 1), jnp.bitwise_and(tile, per_angle - 1)
    return lax.div(tile, jnp.int32(per_angle)), lax.rem(tile, jnp.int32(per_angle))


def entry_bits(word):
    return jnp.bitwise_and(word, SLOT_BIT - 1)


def slot_bits(word):
    return jnp.bitwise_and(lax.shift_right_logical(word, 16), 255)


def away(group, me, groups):
    if groups & (groups - 1) == 0:
        return jnp.bitwise_xor(group, me)
    return lax.rem(group - me + groups, jnp.int32(groups))


def forward_kernel(per_angle, groups, room, live_count, tile_hbm, slot_hbm, volume_hbm, blocks_hbm,
                   partial_out, lists, kept, tile_of, slot_of, volume, volume_b, total, held, open_tile, sems,
                   block_sems, kept_sem):
    entries = blocks_hbm.shape[0]
    slot_count, tile_rows = partial_out.shape[0], volume.shape[0]
    parts = block_sems.shape[0]
    edges = [entries * c // parts for c in range(parts + 1)]
    small = [
        pltpu.make_async_copy(slot_hbm, slot_of, sems.at[0]),
        pltpu.make_async_copy(tile_hbm, tile_of, sems.at[1]),
        pltpu.make_async_copy(volume_hbm, volume, sems.at[2]),
    ]
    large = []
    for c in range(parts):
        part = pl.ds(edges[c], edges[c + 1] - edges[c])
        large.append(pltpu.make_async_copy(blocks_hbm.at[part], held.at[part], block_sems.at[c]))
    keep = pltpu.make_async_copy(blocks_hbm, kept, kept_sem)
    for copy in small + large + [keep]:
        copy.start()
    me = lax.axis_index("angle").astype(jnp.int32)
    total[...] = jnp.zeros_like(total)
    for g in range(groups):
        lists[g] = 0
    for t in range(tile_rows):
        open_tile[t] = -1
    for copy in small:
        copy.wait()
    live = live_count[0]
    for t in range(tile_rows):
        volume_b[t] = volume[t].T.astype(jnp.bfloat16)

    def list_base(g):
        return groups + g * (2 * room)

    def work(e):
        is_live = e < live
        s, t = slot_of[e], tile_of[e]
        total[jnp.where(is_live, s, slot_count)] += dot(held[e], volume_b[t])
        g, row = split_tile(t, per_angle)
        g = away(g, me, groups)
        word = e + s * SLOT_BIT + row * TILE_BIT
        waiting = open_tile[t]
        paired = waiting >= 0
        m = lists[g]
        at = list_base(g) + 2 * m
        lists[at] = waiting
        lists[at + 1] = word
        lists[g] = m + jnp.logical_and(paired, is_live).astype(jnp.int32)
        open_tile[t] = jnp.where(is_live, jnp.where(paired, -1, word), waiting)

    for c in range(parts):
        large[c].wait()

        @pl.when(edges[c] < live)
        def _(c=c):
            for e in range(edges[c], edges[c + 1]):
                work(e)

    for t in range(tile_rows):
        waiting = open_tile[t]
        g = away(split_tile(jnp.int32(t), per_angle)[0], me, groups)
        m = lists[g]
        at = list_base(g) + 2 * m
        lists[at] = waiting
        lists[at + 1] = slot_count * SLOT_BIT
        lists[g] = m + (waiting >= 0).astype(jnp.int32)
    for g in range(groups):
        at = list_base(g) + 2 * lists[g]
        for u in range(BACKWARD_PAIRS):
            lists[at + 2 * u] = per_angle * TILE_BIT
            lists[at + 2 * u + 1] = 0
    for s in range(slot_count):
        partial_out[s] = total[s].T.astype(partial_out.dtype)
    keep.wait()


def project(ray_of, received, total):
    total[...] = jnp.zeros_like(total)
    for r in range(received.shape[0]):
        total[ray_of[r]] += received[r].astype(jnp.float32)


def outgoing_kernel(ray_of, received, sinogram, ray_weight, outgoing, total, rounded):
    project(ray_of, received, total)
    rounded[...] = (ray_weight[...][:, None, :] * (sinogram[...] - total[...])).astype(rounded.dtype)
    for r in range(received.shape[0]):
        outgoing[r] = rounded[ray_of[r]]


def backward_sums(mask, groups, per_angle, lists, kept, returned, rows, total):
    slot_count = returned.shape[0]
    room = (lists.shape[0] - groups) // (2 * groups)
    rows[pl.ds(0, slot_count)] = returned[...]
    rows[slot_count] = jnp.zeros(rows.shape[1:], rows.dtype)
    total[...] = jnp.zeros_like(total)
    first = groups + mask * (2 * room)

    def multiply(i, _):
        for u in range(BACKWARD_PAIRS):
            at = first + 2 * (i * BACKWARD_PAIRS + u)
            one, two = lists[at], lists[at + 1]
            left = jnp.concatenate([rows[slot_bits(one)], rows[slot_bits(two)]], axis=1)
            right = jnp.concatenate([kept[entry_bits(one)], kept[entry_bits(two)]], axis=0)
            total[lax.shift_right_logical(one, 24)] += dot(left, right)
        return 0

    lax.fori_loop(0, ceil_div(lists[mask], BACKWARD_PAIRS), multiply, 0)
    return total[pl.ds(0, per_angle)]


def backward_kernel(mask, groups, lists, kept, returned, out, rows, total):
    out[...] = backward_sums(mask, groups, out.shape[0], lists, kept, returned, rows, total).astype(out.dtype)


def join_kernel(n_recv, share, *refs):
    recv, out = refs[:n_recv], refs[n_recv]
    value = share[...]
    for piece in recv:
        value = value + piece[...].astype(jnp.float32)
    out[...] = value.astype(out.dtype)


def own_kernel(groups, lists, ray_of, kept, returned, received, sinogram, ray_weight, volume_hbm, weight_hbm,
               out, weight_out, residual, rows, volume, weight, total, rays, sems):
    per_angle = out.shape[0]
    mine = pl.ds(lax.axis_index("angle").astype(jnp.int32) * per_angle, per_angle)
    copies = [
        pltpu.make_async_copy(volume_hbm.at[mine], volume, sems.at[0]),
        pltpu.make_async_copy(weight_hbm, weight, sems.at[1]),
    ]
    for copy in copies:
        copy.start()
    project(ray_of, received, rays)
    rays[...] = ray_weight[...][:, None, :] * (sinogram[...] - rays[...])
    away_copy = pltpu.make_async_copy(rays, residual, sems.at[2])
    away_copy.start()
    value = backward_sums(0, groups, per_angle, lists, kept, returned, rows, total)
    for copy in copies:
        copy.wait()
    scale = weight[mine][:, None, :]
    weight_out[...] = scale
    out[...] = volume[...] + scale * value
    away_copy.wait()


def update_kernel(n_recv, own, weight, *refs):
    recv, out = refs[:n_recv], refs[n_recv]
    value = recv[0][...].astype(jnp.float32)
    for piece in recv[1:]:
        value = value + piece[...].astype(jnp.float32)
    out[...] = own[...] + weight[...] * value


def body(volume, blocks, tile_of, slot_of, live_count, ray_of, sinogram, ray_weight, pixel_weight):
    n_region = lax.axis_size("region")
    n_angle = lax.axis_size("angle")
    slot_count = ray_of.shape[0]
    capacity = slot_count // n_region
    ray_rows = sinogram.shape[0]
    tile_rows, slices, pixels = volume.shape
    entries, rays, _ = blocks.shape
    per_angle = tile_rows // n_angle
    f32, bf16, i32 = jnp.float32, jnp.bfloat16, jnp.int32
    room = entries // 2 + per_angle + BACKWARD_PAIRS
    parts = min(FORWARD_PARTS, entries)
    params = pltpu.CompilerParams(vmem_limit_bytes=VMEM_LIMIT)
    in_hbm = functools.partial(pltpu.with_memory_space_constraint, memory_space=pltpu.HBM)
    in_vmem = functools.partial(pltpu.with_memory_space_constraint, memory_space=pltpu.VMEM)
    list_size = n_angle * (2 * room + 1)

    partial_value, lists, kept = pl.pallas_call(
        functools.partial(forward_kernel, per_angle, n_angle, room),
        out_shape=(
            MAYBE_HBM((slot_count, slices, rays), bf16),
            jax.ShapeDtypeStruct((list_size,), i32),
            pltpu.VMEM(blocks.shape, bf16),
        ),
        in_specs=[SMEM_SPEC] + [HBM_SPEC] * 4,
        out_specs=(VMEM_SPEC, SMEM_SPEC, pl.BlockSpec(memory_space=pl.ANY)),
        scratch_shapes=[
            pltpu.SMEM((entries,), i32),
            pltpu.SMEM((entries,), i32),
            pltpu.VMEM((tile_rows, slices, pixels), f32),
            pltpu.VMEM((tile_rows, slices, pixels), bf16),
            pltpu.VMEM((slot_count + 1, slices, rays), f32),
            pltpu.VMEM((entries, rays, pixels), bf16),
            pltpu.SMEM((tile_rows,), i32),
            pltpu.SemaphoreType.DMA((3,)),
            pltpu.SemaphoreType.DMA((parts,)),
            pltpu.SemaphoreType.DMA,
        ],
        compiler_params=params,
        name="forward",
    )(live_count, *[in_hbm(x) for x in (tile_of, slot_of, volume, blocks)])

    received = lax.all_to_all(
        partial_value.reshape((n_region, capacity, slices, rays)), "region", split_axis=0, concat_axis=0, tiled=True
    ).reshape(slot_count, slices, rays)

    outgoing = pl.pallas_call(
        outgoing_kernel,
        out_shape=jax.ShapeDtypeStruct((slot_count, slices, rays), bf16),
        in_specs=[SMEM_SPEC, VMEM_SPEC, VMEM_SPEC, VMEM_SPEC],
        out_specs=VMEM_SPEC,
        scratch_shapes=[
            pltpu.VMEM((ray_rows, slices, rays), f32),
            pltpu.VMEM((ray_rows, slices, rays), bf16),
        ],
        compiler_params=params,
        name="outgoing",
    )(ray_of, received, sinogram, ray_weight)

    returned = lax.all_to_all(
        outgoing.reshape((n_region, capacity, slices, rays)), "region", split_axis=0, concat_axis=0, tiled=True
    ).reshape(slot_count, slices, rays)

    kept = in_vmem(kept)
    tile_shape = (per_angle, slices, pixels)
    work = [pltpu.VMEM((slot_count + 1, slices, rays), bf16), pltpu.VMEM((per_angle + 1, slices, pixels), f32)]

    def backward(mask, rows, out_type):
        return pl.pallas_call(
            functools.partial(backward_kernel, mask, n_angle),
            out_shape=jax.ShapeDtypeStruct(tile_shape, out_type),
            in_specs=[SMEM_SPEC] + [VMEM_SPEC] * 2,
            out_specs=VMEM_SPEC,
            scratch_shapes=work,
            compiler_params=params,
            name=f"backward_{mask}",
        )(lists, kept, rows)

    paired = n_angle & (n_angle - 1) == 0
    inbox = {m: [] for m in range(n_angle)}
    rows = returned
    for mask in range(n_angle - 1, 0, -1):
        recv = inbox[mask]
        share = backward(mask, rows, f32 if recv else bf16)
        if recv:
            share = pl.pallas_call(
                functools.partial(join_kernel, len(recv)),
                out_shape=jax.ShapeDtypeStruct(tile_shape, bf16),
                in_specs=[VMEM_SPEC] * (1 + len(recv)),
                out_specs=VMEM_SPEC,
                compiler_params=params,
                name=f"join_{mask}",
            )(share, *recv)
            share, rows = lax.optimization_barrier((share, rows))
        hop = mask & -mask if paired else mask
        there = [(j, j ^ hop if paired else (j + hop) % n_angle) for j in range(n_angle)]
        inbox[mask ^ hop if paired else 0].append(lax.ppermute(share, "angle", there))
    own, weight, residual = pl.pallas_call(
        functools.partial(own_kernel, n_angle),
        out_shape=(
            jax.ShapeDtypeStruct(tile_shape, f32),
            jax.ShapeDtypeStruct((per_angle, 1, pixels), f32),
            jax.ShapeDtypeStruct((ray_rows, slices, rays), f32),
        ),
        in_specs=[SMEM_SPEC] * 2 + [VMEM_SPEC] * 5 + [HBM_SPEC] * 2,
        out_specs=(VMEM_SPEC, VMEM_SPEC, HBM_SPEC),
        scratch_shapes=[
            work[0],
            pltpu.VMEM(tile_shape, f32),
            pltpu.VMEM(pixel_weight.shape, f32),
            work[1],
            pltpu.VMEM((ray_rows, slices, rays), f32),
            pltpu.SemaphoreType.DMA((3,)),
        ],
        compiler_params=params,
        name="own",
    )(lists, ray_of, kept, rows, received, sinogram, ray_weight, in_hbm(volume), in_hbm(pixel_weight))
    recv = inbox[0]
    updated = pl.pallas_call(
        functools.partial(update_kernel, len(recv)),
        out_shape=jax.ShapeDtypeStruct((per_angle, slices, pixels), f32),
        in_specs=[VMEM_SPEC] * (len(recv) + 2),
        out_specs=VMEM_SPEC,
        compiler_params=params,
        name="update",
    )(own, weight, *recv)
    return (updated, residual)


def solution(mesh):
    placed = (
        P("region", None, None),
        P(("region", "angle"), None, None),
        P(("region", "angle")),
        P(("region", "angle")),
        P(("region", "angle")),
        P(("region", "angle")),
        P(("region", "angle"), None, None),
        P(("region", "angle"), None),
        P("region", None),
    )
    return jax.shard_map(
        body,
        mesh=mesh,
        in_specs=placed,
        out_specs=(P(("region", "angle"), None, None), P(("region", "angle"), None, None)),
        check_vma=False,
    )
```

time: 50.4 us -> 47.4 us (0.940)
  Pallas kernels: 18 us -> 15.1 us
  waiting for transfers between devices: 2.93 us -> 0.65 us
  blocking collectives: 27 us -> 28 us
  starting transfers between devices: 1.23 us -> 1.9 us
    ppermute x3, waiting for transfers between devices: 2.93 us -> 0.65 us  [body(): lax.ppermute(share, 'angle', there)]
    pallas_call x1, Pallas kernels: 8.37 us -> 6.94 us  [body(): pl.pallas_call(functools.partial(forward_kernel, per_angle, n_angle, room...]
    pallas_call x4 -> x5, Pallas kernels: 6.92 us -> 5.59 us  [the longest x3 4.8 us: backward(): pl.pallas_call(functools.partial(backward_kernel, mask, n_angle), out_sha...]
    all_to_all x1, blocking collectives: 15.1 us -> 16 us  [body(): lax.all_to_all(partial_value.reshape((n_region, capacity, slices, rays)),...]
    ppermute x3, starting transfers between devices: 1.23 us -> 1.9 us  [body(): lax.ppermute(share, 'angle', there)]
where the time goes in v3:
time: 47.4 us; the launch traced here: 47.1 us
  blocking collectives  28 us (59%)
  Pallas kernels  15.1 us (32%)
  starting transfers between devices  1.9 us (4%)
  between operations  1.44 us (3%)
  waiting for transfers between devices  0.65 us (1%)
    all_to_all x1, blocking collectives, body(): lax.all_to_all(partial_value.reshape((n_region, capacity, slices, rays)),...  16 us
    all_to_all x1, blocking collectives, body(): lax.all_to_all(outgoing.reshape((n_region, capacity, slices, rays)), 'reg...  11.9 us
    pallas_call x1, Pallas kernels, body(): pl.pallas_call(functools.partial(forward_kernel, per_angle, n_angle, room...  6.94 us
    pallas_call x3, Pallas kernels, backward(): pl.pallas_call(functools.partial(backward_kernel, mask, n_angle), out_sha...  4.8 us
    ppermute x3, starting transfers between devices, body(): lax.ppermute(share, 'angle', there)  1.9 us
    pallas_call x1, Pallas kernels, body(): pl.pallas_call(functools.partial(own_kernel, n_angle), out_shape=(jax.Sha...  1.86 us
  transfers between devices with their start and end apart: 3, of which 1 were waited for; matrix products, arithmetic and copies ran while one was open for 0% of the time, Pallas kernels for 11%

profile of v3, /device:TPU:0, one launch (start us, length us, event | category | flops | bytes accessed | tf_op | source)
XLA Modules:
  0.0 47.1 jit_solution(13303166995403498296)
XLA Ops:
  0.6 0.0 copy-start.2
  0.6 0.0 copy-start
  0.7 0.0 copy-start.1
  1.4 6.9 %forward.1 = (bf16[8,128,128]{2,1,0:T(8,128)(2,1)S(1)}, s32[1188]{0:T(1024)S(1)}, bf16[256,128,128]{2,1,0:T(8,128)(2,1)S(1)}) custom-call(s32[1]{0:T(128)S(6)} %copy.13.live_count, s32[256]{0:T(256)} %tile_hbm.1, s32[256]{0:T(256)} %slot_hbm.1, f32[16,128,128]{2,1,0:T(8,128)} %volume_hbm.3, bf16[256,128,128]{2,1,0:T(8,128)(2,1)} %blocks_hbm.1), custom_call_target="tpu_custom_call" | custom-call | tf_op jit(solution)/shard_map/forward/pallas_call | solution.py:219
  8.3 16.0 %all_to_all.10 = bf16[8,1,128,128]{3,2,1,0:T(8,128)(2,1)S(1)} all-to-all(bf16[8,1,128,128]{3,2,1,0:T(8,128)(2,1)S(1)} %bitcast.15), channel_id=1, replica_groups=mesh['region'=8,'angle'=4] {'region'}, dimensions={0} | all-to-all | bytes 524288 | tf_op jit(solution)/shard_map/all_to_all | solution.py:244
  24.3 0.0 copy-done.2
  24.3 0.0 copy-done
  24.3 0.0 copy-done.1
  24.3 0.8 %outgoing.1 = bf16[8,128,128]{2,1,0:T(8,128)(2,1)S(1)} custom-call(s32[8]{0:T(128)S(1)} %copy-done.2, bf16[8,128,128]{2,1,0:T(8,128)(2,1)S(1)} %bitcast.12, f32[8,128,128]{2,1,0:T(8,128)S(1)} %copy-done, f32[8,128]{1,0:T(8,128)S(1)} %copy-done.1), custom_call_target="tpu_custom_call" | custom-call | tf_op jit(solution)/shard_map/outgoing/pallas_call | solution.py:248
  25.1 11.9 %all_to_all.11 = bf16[8,1,128,128]{3,2,1,0:T(8,128)(2,1)S(1)} all-to-all(bf16[8,1,128,128]{3,2,1,0:T(8,128)(2,1)S(1)} %bitcast.14), channel_id=1, replica_groups=mesh['region'=8,'angle'=4] {'region'}, dimensions={0} | all-to-all | bytes 524288 | tf_op jit(solution)/shard_map/all_to_all | solution.py:261
  37.0 1.6 %backward_3.1 = bf16[4,128,128]{2,1,0:T(8,128)(2,1)S(1)} custom-call(s32[1188]{0:T(1024)S(1)} %get-tuple-element.10.lists, bf16[256,128,128]{2,1,0:T(8,128)(2,1)S(1)} %get-tuple-element.11.kept, bf16[8,128,128]{2,1,0:T(8,128)(2,1)S(1)} %bitcast.8), custom_call_target="tpu_custom_call" | custom-call | tf_op jit(solution)/shard_map/backward_3/pallas_call | solution.py:270
  38.7 0.1 collective-permute-start
  38.7 1.6 %backward_2.1.share = f32[4,128,128]{2,1,0:T(8,128)S(1)} custom-call(s32[1188]{0:T(1024)S(1)} %get-tuple-element.10.lists, bf16[256,128,128]{2,1,0:T(8,128)(2,1)S(1)} %get-tuple-element.11.kept, bf16[8,128,128]{2,1,0:T(8,128)(2,1)S(1)} %bitcast.9), custom_call_target="tpu_custom_call" | custom-call | tf_op jit(solution)/shard_map/backward_2/pallas_call | solution.py:270
  40.3 0.0 collective-permute-done.refs_0_
  40.4 1.6 %collective-permute-start.1 = (bf16[4,128,128]{2,1,0:T(8,128)(2,1)S(1)}, bf16[4,128,128]{2,1,0:T(8,128)(2,1)S(1)}, u32[]{:S(2)}, u32[]{:S(2)}) collective-permute-start(bf16[4,128,128]{2,1,0:T(8,128)(2,1)S(1)} %join_2.1), channel_id=1, source_target_pairs={{0,2},{1,3},{2,0},{3,1},{4,6},{5,7},{6,4},{7,5},{8,10},{9,11},{10,... | collective-permute-start | bytes 393224 | tf_op jit(solution)/shard_map/ppermute | solution.py:298
  41.9 1.6 %backward_1.1 = bf16[4,128,128]{2,1,0:T(8,128)(2,1)S(1)} custom-call(s32[1188]{0:T(1024)S(1)} %get-tuple-element.10.lists, bf16[256,128,128]{2,1,0:T(8,128)(2,1)S(1)} %get-tuple-element.11.kept, bf16[8,128,128]{2,1,0:T(8,128)(2,1)S(1)} %bitcast.10), custom_call_target="tpu_custom_call" | custom-call | tf_op jit(solution)/shard_map/backward_1/pallas_call | solution.py:270
  43.5 0.3 collective-permute-start.2
  43.8 1.9 %own.1 = (f32[4,128,128]{2,1,0:T(8,128)S(1)}, f32[4,1,128]{2,1,0:T(1,128)S(1)}, f32[8,128,128]{2,1,0:T(8,128)}) custom-call(s32[1188]{0:T(1024)S(1)} %get-tuple-element.10.lists, s32[8]{0:T(128)S(1)} %copy-done.2, bf16[256,128,128]{2,1,0:T(8,128)(2,1)S(1)} %get-tuple-element.11.kept, bf16[8,128,128]{2,1,0:T(8,128)(2,1)S(1)} %bitcast.11, ...), custom_call_target="tpu_custom_call" | custom-call | tf_op jit(solution)/shard_map/own/pallas_call | solution.py:299
  45.7 0.6 %collective-permute-done.1.refs_0_ = bf16[4,128,128]{2,1,0:T(8,128)(2,1)S(1)} collective-permute-done((bf16[4,128,128]{2,1,0:T(8,128)(2,1)S(1)}, bf16[4,128,128]{2,1,0:T(8,128)(2,1)S(1)}, u32[]{:S(2)}, u32[]{:S(2)}) %collective-permute-start.1) | collective-permute-done | bytes 131104 | tf_op jit(solution)/shard_map/ppermute | solution.py:298
  46.3 0.0 collective-permute-done.2.refs_1_
  46.4 0.7 %update.1 = f32[4,128,128]{2,1,0:T(8,128)} custom-call(f32[4,128,128]{2,1,0:T(8,128)S(1)} %get-tuple-element.14.own, f32[4,1,128]{2,1,0:T(1,128)S(1)} %get-tuple-element.15.weight, bf16[4,128,128]{2,1,0:T(8,128)(2,1)S(1)} %collective-permute-done.1.refs_0_, bf16[4,128,128]{2,1,0:T(8,128)(2,1)S(1)} %collective-permute-done.2.refs_1_), custom_call_target="tpu_custom_call" | custom-call | tf_op jit(solution)/shard_map/update/pallas_call | solution.py:320
  (1 shorter events, 0.0 us)
Async XLA Ops:
  0.6 23.7 %copy-start.2 = (s32[8]{0:T(128)S(1)}, s32[8]{0:T(128)}, u32[]{:S(2)}) copy-start(s32[8]{0:T(128)} %ray_of.3) | copy-start | bytes 100
  0.6 23.7 %copy-start = (f32[8,128,128]{2,1,0:T(8,128)S(1)}, f32[8,128,128]{2,1,0:T(8,128)}, u32[]{:S(2)}) copy-start(f32[8,128,128]{2,1,0:T(8,128)} %sinogram.3) | copy-start | bytes 1572868
  0.7 23.7 %copy-start.1 = (f32[8,128]{1,0:T(8,128)S(1)}, f32[8,128]{1,0:T(8,128)}, u32[]{:S(2)}) copy-start(f32[8,128]{1,0:T(8,128)} %ray_weight.3) | copy-start | bytes 12292
  38.7 1.7 %collective-permute-start = (bf16[4,128,128]{2,1,0:T(8,128)(2,1)S(1)}, bf16[4,128,128]{2,1,0:T(8,128)(2,1)S(1)}, u32[]{:S(2)}, u32[]{:S(2)}) collective-permute-start(bf16[4,128,128]{2,1,0:T(8,128)(2,1)S(1)} %backward_3.1), channel_id=1, source_target_pairs={{0,1},{1,0},{2,3},{3,2},{4,5},{5,4},{6,7},{7,6},{8,9},{9,8},{10,11... | collective-permute-start | bytes 393224 | tf_op jit(solution)/shard_map/ppermute | solution.py:298
  40.4 6.0 %collective-permute-start.1 = (bf16[4,128,128]{2,1,0:T(8,128)(2,1)S(1)}, bf16[4,128,128]{2,1,0:T(8,128)(2,1)S(1)}, u32[]{:S(2)}, u32[]{:S(2)}) collective-permute-start(bf16[4,128,128]{2,1,0:T(8,128)(2,1)S(1)} %join_2.1), channel_id=1, source_target_pairs={{0,2},{1,3},{2,0},{3,1},{4,6},{5,7},{6,4},{7,5},{8,10},{9,11},{10,... | collective-permute-start | bytes 393224 | tf_op jit(solution)/shard_map/ppermute | solution.py:298
  43.5 2.8 %collective-permute-start.2 = (bf16[4,128,128]{2,1,0:T(8,128)(2,1)S(1)}, bf16[4,128,128]{2,1,0:T(8,128)(2,1)S(1)}, u32[]{:S(2)}, u32[]{:S(2)}) collective-permute-start(bf16[4,128,128]{2,1,0:T(8,128)(2,1)S(1)} %backward_1.1), channel_id=1, source_target_pairs={{0,1},{1,0},{2,3},{3,2},{4,5},{5,4},{6,7},{7,6},{8,9},{9,8},{10,11... | collective-permute-start | bytes 393224 | tf_op jit(solution)/shard_map/ppermute | solution.py:298

commit v4 on v3

--- a/solution.py
+++ b/solution.py
@@ -46,8 +46,8 @@
     return lax.rem(group - me + groups, jnp.int32(groups))
 
 
-def forward_kernel(per_angle, groups, room, live_count, tile_hbm, slot_hbm, volume_hbm, blocks_hbm,
-                   partial_out, lists, kept, tile_of, slot_of, volume, volume_b, total, held, open_tile, sems,
+def forward_kernel(per_angle, groups, room, live_count, tile_hbm, slot_hbm, ray_hbm, volume_hbm, blocks_hbm,
+                   partial_out, lists, rays, kept, tile_of, slot_of, volume, volume_b, total, held, open_tile, sems,
                    block_sems, kept_sem):
     entries = blocks_hbm.shape[0]
     slot_count, tile_rows = partial_out.shape[0], volume.shape[0]
@@ -57,6 +57,7 @@
         pltpu.make_async_copy(slot_hbm, slot_of, sems.at[0]),
         pltpu.make_async_copy(tile_hbm, tile_of, sems.at[1]),
         pltpu.make_async_copy(volume_hbm, volume, sems.at[2]),
+        pltpu.make_async_copy(ray_hbm, rays, sems.at[3]),
     ]
     large = []
     for c in range(parts):
@@ -216,15 +217,16 @@
     in_vmem = functools.partial(pltpu.with_memory_space_constraint, memory_space=pltpu.VMEM)
     list_size = n_angle * (2 * room + 1)
 
-    partial_value, lists, kept = pl.pallas_call(
+    partial_value, lists, rays_of, kept = pl.pallas_call(
         functools.partial(forward_kernel, per_angle, n_angle, room),
         out_shape=(
             MAYBE_HBM((slot_count, slices, rays), bf16),
-            jax.ShapeDtypeStruct((list_size,), i32),
+            pltpu.SMEM((list_size,), i32),
+            pltpu.SMEM((slot_count,), i32),
             pltpu.VMEM(blocks.shape, bf16),
         ),
-        in_specs=[SMEM_SPEC] + [HBM_SPEC] * 4,
-        out_specs=(VMEM_SPEC, SMEM_SPEC, pl.BlockSpec(memory_space=pl.ANY)),
+        in_specs=[SMEM_SPEC] + [HBM_SPEC] * 5,
+        out_specs=(VMEM_SPEC, SMEM_SPEC, SMEM_SPEC, pl.BlockSpec(memory_space=pl.ANY)),
         scratch_shapes=[
             pltpu.SMEM((entries,), i32),
             pltpu.SMEM((entries,), i32),
@@ -233,13 +235,13 @@
             pltpu.VMEM((slot_count + 1, slices, rays), f32),
             pltpu.VMEM((entries, rays, pixels), bf16),
             pltpu.SMEM((tile_rows,), i32),
-            pltpu.SemaphoreType.DMA((3,)),
+            pltpu.SemaphoreType.DMA((4,)),
             pltpu.SemaphoreType.DMA((parts,)),
             pltpu.SemaphoreType.DMA,
         ],
         compiler_params=params,
         name="forward",
-    )(live_count, *[in_hbm(x) for x in (tile_of, slot_of, volume, blocks)])
+    )(live_count, *[in_hbm(x) for x in (tile_of, slot_of, ray_of, volume, blocks)])
 
     received = lax.all_to_all(
         partial_value.reshape((n_region, capacity, slices, rays)), "region", split_axis=0, concat_axis=0, tiled=True
@@ -256,7 +258,7 @@
         ],
         compiler_params=params,
         name="outgoing",
-    )(ray_of, received, sinogram, ray_weight)
+    )(rays_of, received, sinogram, ray_weight)
 
     returned = lax.all_to_all(
         outgoing.reshape((n_region, capacity, slices, rays)), "region", split_axis=0, concat_axis=0, tiled=True
@@ -315,7 +317,7 @@
         ],
         compiler_params=params,
         name="own",
-    )(lists, ray_of, kept, rows, received, sinogram, ray_weight, in_hbm(volume), in_hbm(pixel_weight))
+    )(lists, rays_of, kept, rows, received, sinogram, ray_weight, in_hbm(volume), in_hbm(pixel_weight))
     recv = inbox[0]
     updated = pl.pallas_call(
         functools.partial(update_kernel, len(recv)),

time: 47.4 us -> 44.9 us (0.947)
  Pallas kernels: 15.1 us -> 11.3 us
  waiting for transfers between devices: 0.65 us -> 2.14 us
    pallas_call x3, Pallas kernels: 4.8 us -> 2.88 us  [backward(): pl.pallas_call(functools.partial(backward_kernel, mask, n_angle), out_sha...]
    ppermute x3, waiting for transfers between devices: 0.65 us -> 2.14 us  [body(): lax.ppermute(share, 'angle', there)]
    pallas_call x1, Pallas kernels: 6.94 us -> 6.22 us  [body(): pl.pallas_call(functools.partial(forward_kernel, per_angle, n_angle, room...]
    pallas_call x1, Pallas kernels: 1.86 us -> 1.22 us  [body(): pl.pallas_call(functools.partial(own_kernel, n_angle), out_shape=(jax.Sha...]
    pallas_call x1, Pallas kernels: 0.76 us -> 0.21 us  [body(): pl.pallas_call(outgoing_kernel, out_shape=jax.ShapeDtypeStruct((slot_coun...]
  transfers between devices with their start and end apart: 3 -> 3, of which waited for: 1 -> 2; matrix products, arithmetic and copies ran while one was open for 0% -> 0% of each run, Pallas kernels for 11% -> 7%
where the time goes in v4:
time: 44.9 us; the launch traced here: 44.5 us
  blocking collectives  27.9 us (62%)
  Pallas kernels  11.3 us (25%)
  waiting for transfers between devices  2.14 us (5%)
  starting transfers between devices  1.7 us (4%)
  between operations  1.42 us (3%)
    all_to_all x1, blocking collectives, body(): lax.all_to_all(partial_value.reshape((n_region, capacity, slices, rays)),...  16 us
    all_to_all x1, blocking collectives, body(): lax.all_to_all(outgoing.reshape((n_region, capacity, slices, rays)), 'reg...  12 us
    pallas_call x1, Pallas kernels, body(): pl.pallas_call(functools.partial(forward_kernel, per_angle, n_angle, room...  6.22 us
    pallas_call x3, Pallas kernels, backward(): pl.pallas_call(functools.partial(backward_kernel, mask, n_angle), out_sha...  2.88 us
    ppermute x3, waiting for transfers between devices, body(): lax.ppermute(share, 'angle', there)  2.14 us
    ppermute x3, starting transfers between devices, body(): lax.ppermute(share, 'angle', there)  1.7 us
    pallas_call x1, Pallas kernels, body(): pl.pallas_call(functools.partial(own_kernel, n_angle), out_shape=(jax.Sha...  1.22 us
  transfers between devices with their start and end apart: 3, of which 2 were waited for; matrix products, arithmetic and copies ran while one was open for 0% of the time, Pallas kernels for 7%

profile of v4, /device:TPU:0, one launch (start us, length us, event | category | flops | bytes accessed | tf_op | source)
XLA Modules:
  0.0 44.5 jit_solution(16055471434633943388)
XLA Ops:
  0.6 0.0 copy-start
  0.6 0.0 copy-start.1
  1.4 6.2 %forward.1 = (bf16[8,128,128]{2,1,0:T(8,128)(2,1)S(1)}, s32[1188]{0:T(1024)S(4)}, s32[8]{0:T(128)S(4)}, bf16[256,128,128]{2,1,0:T(8,128)(2,1)S(1)}) custom-call(s32[1]{0:T(128)S(6)} %copy.13.live_count, s32[256]{0:T(256)} %tile_hbm.1, s32[256]{0:T(256)} %slot_hbm.1, s32[8]{0:T(128)} %ray_hbm.1, f32[16,128,128]{2,1,0:T(8,128)} %volume_hbm.3, ...), custom_call_target="tpu_custom_call" | custom-call | tf_op jit(solution)/shard_map/forward/pallas_call | solution.py:220
  7.6 16.0 %all_to_all.10 = bf16[8,1,128,128]{3,2,1,0:T(8,128)(2,1)S(1)} all-to-all(bf16[8,1,128,128]{3,2,1,0:T(8,128)(2,1)S(1)} %bitcast.15), channel_id=1, replica_groups=mesh['region'=8,'angle'=4] {'region'}, dimensions={0} | all-to-all | bytes 524288 | tf_op jit(solution)/shard_map/all_to_all | solution.py:246
  23.6 0.0 copy-done
  23.6 0.0 copy-done.1
  23.6 0.2 outgoing.1
  23.8 12.0 %all_to_all.11 = bf16[8,1,128,128]{3,2,1,0:T(8,128)(2,1)S(1)} all-to-all(bf16[8,1,128,128]{3,2,1,0:T(8,128)(2,1)S(1)} %bitcast.14), channel_id=1, replica_groups=mesh['region'=8,'angle'=4] {'region'}, dimensions={0} | all-to-all | bytes 524288 | tf_op jit(solution)/shard_map/all_to_all | solution.py:263
  35.7 1.0 %backward_3.1 = bf16[4,128,128]{2,1,0:T(8,128)(2,1)S(1)} custom-call(s32[1188]{0:T(1024)S(4)} %get-tuple-element.11.lists, bf16[256,128,128]{2,1,0:T(8,128)(2,1)S(1)} %get-tuple-element.13.kept, bf16[8,128,128]{2,1,0:T(8,128)(2,1)S(1)} %bitcast.8), custom_call_target="tpu_custom_call" | custom-call | tf_op jit(solution)/shard_map/backward_3/pallas_call | solution.py:272
  36.7 0.1 collective-permute-start
  36.8 1.0 %backward_2.1.share = f32[4,128,128]{2,1,0:T(8,128)S(1)} custom-call(s32[1188]{0:T(1024)S(4)} %get-tuple-element.11.lists, bf16[256,128,128]{2,1,0:T(8,128)(2,1)S(1)} %get-tuple-element.13.kept, bf16[8,128,128]{2,1,0:T(8,128)(2,1)S(1)} %bitcast.9), custom_call_target="tpu_custom_call" | custom-call | tf_op jit(solution)/shard_map/backward_2/pallas_call | solution.py:272
  37.8 0.4 collective-permute-done.refs_0_
  38.2 1.6 %collective-permute-start.1 = (bf16[4,128,128]{2,1,0:T(8,128)(2,1)S(1)}, bf16[4,128,128]{2,1,0:T(8,128)(2,1)S(1)}, u32[]{:S(2)}, u32[]{:S(2)}) collective-permute-start(bf16[4,128,128]{2,1,0:T(8,128)(2,1)S(1)} %join_2.1), channel_id=1, source_target_pairs={{0,2},{1,3},{2,0},{3,1},{4,6},{5,7},{6,4},{7,5},{8,10},{9,11},{10,... | collective-permute-start | bytes 393224 | tf_op jit(solution)/shard_map/ppermute | solution.py:300
  39.7 1.0 %backward_1.1 = bf16[4,128,128]{2,1,0:T(8,128)(2,1)S(1)} custom-call(s32[1188]{0:T(1024)S(4)} %get-tuple-element.11.lists, bf16[256,128,128]{2,1,0:T(8,128)(2,1)S(1)} %get-tuple-element.13.kept, bf16[8,128,128]{2,1,0:T(8,128)(2,1)S(1)} %bitcast.10), custom_call_target="tpu_custom_call" | custom-call | tf_op jit(solution)/shard_map/backward_1/pallas_call | solution.py:272
  40.7 0.1 collective-permute-start.2
  40.8 1.2 %own.1 = (f32[4,128,128]{2,1,0:T(8,128)S(1)}, f32[4,1,128]{2,1,0:T(1,128)S(1)}, f32[8,128,128]{2,1,0:T(8,128)}) custom-call(s32[1188]{0:T(1024)S(4)} %get-tuple-element.11.lists, s32[8]{0:T(128)S(4)} %get-tuple-element.12.ray_of, bf16[256,128,128]{2,1,0:T(8,128)(2,1)S(1)} %get-tuple-element.13.kept, bf16[8,128,128]{2,1,0:T(8,128)(2,1)S(1)} %bitcast.11, ...), custom_call_target="tpu_custom_call" | custom-call | tf_op jit(solution)/shard_map/own/pallas_call | solution.py:301
  42.0 1.8 %collective-permute-done.1.refs_0_ = bf16[4,128,128]{2,1,0:T(8,128)(2,1)S(1)} collective-permute-done((bf16[4,128,128]{2,1,0:T(8,128)(2,1)S(1)}, bf16[4,128,128]{2,1,0:T(8,128)(2,1)S(1)}, u32[]{:S(2)}, u32[]{:S(2)}) %collective-permute-start.1) | collective-permute-done | bytes 131104 | tf_op jit(solution)/shard_map/ppermute | solution.py:300
  43.8 0.0 collective-permute-done.2.refs_1_
  43.8 0.8 %update.1 = f32[4,128,128]{2,1,0:T(8,128)} custom-call(f32[4,128,128]{2,1,0:T(8,128)S(1)} %get-tuple-element.16.own, f32[4,1,128]{2,1,0:T(1,128)S(1)} %get-tuple-element.17.weight, bf16[4,128,128]{2,1,0:T(8,128)(2,1)S(1)} %collective-permute-done.1.refs_0_, bf16[4,128,128]{2,1,0:T(8,128)(2,1)S(1)} %collective-permute-done.2.refs_1_), custom_call_target="tpu_custom_call" | custom-call | tf_op jit(solution)/shard_map/update/pallas_call | solution.py:322
  (1 shorter events, 0.0 us)
Async XLA Ops:
  0.6 22.9 %copy-start = (f32[8,128,128]{2,1,0:T(8,128)S(1)}, f32[8,128,128]{2,1,0:T(8,128)}, u32[]{:S(2)}) copy-start(f32[8,128,128]{2,1,0:T(8,128)} %sinogram.3) | copy-start | bytes 1572868
  0.6 22.9 %copy-start.1 = (f32[8,128]{1,0:T(8,128)S(1)}, f32[8,128]{1,0:T(8,128)}, u32[]{:S(2)}) copy-start(f32[8,128]{1,0:T(8,128)} %ray_weight.3) | copy-start | bytes 12292
  36.7 1.4 %collective-permute-start = (bf16[4,128,128]{2,1,0:T(8,128)(2,1)S(1)}, bf16[4,128,128]{2,1,0:T(8,128)(2,1)S(1)}, u32[]{:S(2)}, u32[]{:S(2)}) collective-permute-start(bf16[4,128,128]{2,1,0:T(8,128)(2,1)S(1)} %backward_3.1), channel_id=1, source_target_pairs={{0,1},{1,0},{2,3},{3,2},{4,5},{5,4},{6,7},{7,6},{8,9},{9,8},{10,11... | collective-permute-start | bytes 393224 | tf_op jit(solution)/shard_map/ppermute | solution.py:300
  38.2 5.6 %collective-permute-start.1 = (bf16[4,128,128]{2,1,0:T(8,128)(2,1)S(1)}, bf16[4,128,128]{2,1,0:T(8,128)(2,1)S(1)}, u32[]{:S(2)}, u32[]{:S(2)}) collective-permute-start(bf16[4,128,128]{2,1,0:T(8,128)(2,1)S(1)} %join_2.1), channel_id=1, source_target_pairs={{0,2},{1,3},{2,0},{3,1},{4,6},{5,7},{6,4},{7,5},{8,10},{9,11},{10,... | collective-permute-start | bytes 393224 | tf_op jit(solution)/shard_map/ppermute | solution.py:300
  40.7 3.1 %collective-permute-start.2 = (bf16[4,128,128]{2,1,0:T(8,128)(2,1)S(1)}, bf16[4,128,128]{2,1,0:T(8,128)(2,1)S(1)}, u32[]{:S(2)}, u32[]{:S(2)}) collective-permute-start(bf16[4,128,128]{2,1,0:T(8,128)(2,1)S(1)} %backward_1.1), channel_id=1, source_target_pairs={{0,1},{1,0},{2,3},{3,2},{4,5},{5,4},{6,7},{7,6},{8,9},{9,8},{10,11... | collective-permute-start | bytes 393224 | tf_op jit(solution)/shard_map/ppermute | solution.py:300

commit v5 on v4

--- a/solution.py
+++ b/solution.py
@@ -7,7 +7,7 @@
 from jax.experimental.pallas import tpu as pltpu
 from jax.sharding import PartitionSpec as P
 
-FORWARD_PARTS = 2
+FORWARD_PARTS = 3
 BACKWARD_PAIRS = 16
 SLOT_BIT = 1 << 16
 TILE_BIT = 1 << 24
@@ -46,9 +46,8 @@
     return lax.rem(group - me + groups, jnp.int32(groups))
 
 
-def forward_kernel(per_angle, groups, room, live_count, tile_hbm, slot_hbm, ray_hbm, volume_hbm, blocks_hbm,
-                   partial_out, lists, rays, kept, tile_of, slot_of, volume, volume_b, total, held, open_tile, sems,
-                   block_sems, kept_sem):
+def forward_kernel(per_angle, groups, room, live_count, tile_hbm, slot_hbm, ray_hbm, volume_hbm, blocks_hbm, held,
+                   partial_out, lists, rays, kept, tile_of, slot_of, volume, volume_b, total, open_tile, sems, block_sems):
     entries = blocks_hbm.shape[0]
     slot_count, tile_rows = partial_out.shape[0], volume.shape[0]
     parts = block_sems.shape[0]
@@ -62,9 +61,8 @@
     large = []
     for c in range(parts):
         part = pl.ds(edges[c], edges[c + 1] - edges[c])
-        large.append(pltpu.make_async_copy(blocks_hbm.at[part], held.at[part], block_sems.at[c]))
-    keep = pltpu.make_async_copy(blocks_hbm, kept, kept_sem)
-    for copy in small + large + [keep]:
+        large.append(pltpu.make_async_copy(blocks_hbm.at[part], kept.at[part], block_sems.at[c]))
+    for copy in small + large:
         copy.start()
     me = lax.axis_index("angle").astype(jnp.int32)
     total[...] = jnp.zeros_like(total)
@@ -120,7 +118,6 @@
             lists[at + 2 * u + 1] = 0
     for s in range(slot_count):
         partial_out[s] = total[s].T.astype(partial_out.dtype)
-    keep.wait()
 
 
 def project(ray_of, received, total):
@@ -217,6 +214,13 @@
     in_vmem = functools.partial(pltpu.with_memory_space_constraint, memory_space=pltpu.VMEM)
     list_size = n_angle * (2 * room + 1)
 
+    space = pl.pallas_call(
+        lambda _: None,
+        out_shape=pltpu.VMEM(blocks.shape, bf16),
+        out_specs=pl.BlockSpec(memory_space=pl.ANY),
+        compiler_params=params,
+        name="space",
+    )()
     partial_value, lists, rays_of, kept = pl.pallas_call(
         functools.partial(forward_kernel, per_angle, n_angle, room),
         out_shape=(
@@ -225,7 +229,7 @@
             pltpu.SMEM((slot_count,), i32),
             pltpu.VMEM(blocks.shape, bf16),
         ),
-        in_specs=[SMEM_SPEC] + [HBM_SPEC] * 5,
+        in_specs=[SMEM_SPEC] + [HBM_SPEC] * 5 + [VMEM_SPEC],
         out_specs=(VMEM_SPEC, SMEM_SPEC, SMEM_SPEC, pl.BlockSpec(memory_space=pl.ANY)),
         scratch_shapes=[
             pltpu.SMEM((entries,), i32),
@@ -233,15 +237,14 @@
             pltpu.VMEM((tile_rows, slices, pixels), f32),
             pltpu.VMEM((tile_rows, slices, pixels), bf16),
             pltpu.VMEM((slot_count + 1, slices, rays), f32),
-            pltpu.VMEM((entries, rays, pixels), bf16),
             pltpu.SMEM((tile_rows,), i32),
             pltpu.SemaphoreType.DMA((4,)),
             pltpu.SemaphoreType.DMA((parts,)),
-            pltpu.SemaphoreType.DMA,
         ],
+        input_output_aliases={6: 3},
         compiler_params=params,
         name="forward",
-    )(live_count, *[in_hbm(x) for x in (tile_of, slot_of, ray_of, volume, blocks)])
+    )(live_count, *[in_hbm(x) for x in (tile_of, slot_of, ray_of, volume, blocks)], in_vmem(space))
 
     received = lax.all_to_all(
         partial_value.reshape((n_region, capacity, slices, rays)), "region", split_axis=0, concat_axis=0, tiled=True
@@ -282,7 +285,7 @@
     paired = n_angle & (n_angle - 1) == 0
     inbox = {m: [] for m in range(n_angle)}
     rows = returned
-    for mask in range(n_angle - 1, 0, -1):
+    def send(mask, rows):
         recv = inbox[mask]
         share = backward(mask, rows, f32 if recv else bf16)
         if recv:
@@ -298,6 +301,10 @@
         hop = mask & -mask if paired else mask
         there = [(j, j ^ hop if paired else (j + hop) % n_angle) for j in range(n_angle)]
         inbox[mask ^ hop if paired else 0].append(lax.ppermute(share, "angle", there))
+        return rows
+
+    for mask in range(n_angle - 1, 1, -1):
+        rows = send(mask, rows)
     own, weight, residual = pl.pallas_call(
         functools.partial(own_kernel, n_angle),
         out_shape=(
@@ -318,6 +325,8 @@
         compiler_params=params,
         name="own",
     )(lists, rays_of, kept, rows, received, sinogram, ray_weight, in_hbm(volume), in_hbm(pixel_weight))
+    rows, own = lax.optimization_barrier((rows, own))
+    send(1, rows)
     recv = inbox[0]
     updated = pl.pallas_call(
         functools.partial(update_kernel, len(recv)),

time: 44.9 us -> 44.7 us (level); the launches traced: 44.5 us -> 44.9 us
  starting transfers between devices: 1.7 us -> 0.36 us
  waiting for transfers between devices: 2.14 us -> 3.48 us
  blocking collectives: 27.9 us -> 28.5 us
    ppermute x3, starting transfers between devices: 1.7 us -> 0.36 us  [send(): lax.ppermute(share, 'angle', there)]
    ppermute x3, waiting for transfers between devices: 2.14 us -> 3.48 us  [send(): lax.ppermute(share, 'angle', there)]
    all_to_all x1, blocking collectives: 12 us -> 12.6 us  [body(): lax.all_to_all(outgoing.reshape((n_region, capacity, slices, rays)), 'reg...]
where the time goes in v5:
time: 44.7 us; the launch traced here: 44.9 us
  blocking collectives  28.5 us (64%)
  Pallas kernels  11.1 us (25%)
  waiting for transfers between devices  3.48 us (8%)
  between operations  1.37 us (3%)
    all_to_all x1, blocking collectives, body(): lax.all_to_all(partial_value.reshape((n_region, capacity, slices, rays)),...  16 us
    all_to_all x1, blocking collectives, body(): lax.all_to_all(outgoing.reshape((n_region, capacity, slices, rays)), 'reg...  12.6 us
    pallas_call x1, Pallas kernels, body(): pl.pallas_call(functools.partial(forward_kernel, per_angle, n_angle, room...  6.01 us
    ppermute x3, waiting for transfers between devices, send(): lax.ppermute(share, 'angle', there)  3.48 us
    pallas_call x3, Pallas kernels, backward(): pl.pallas_call(functools.partial(backward_kernel, mask, n_angle), out_sha...  2.89 us
    pallas_call x1, Pallas kernels, body(): pl.pallas_call(functools.partial(own_kernel, n_angle), out_shape=(jax.Sha...  1.22 us
  transfers between devices with their start and end apart: 3, of which 2 were waited for; matrix products, arithmetic and copies ran while one was open for 0% of the time, Pallas kernels for 7%

profile of v5, /device:TPU:0, one launch (start us, length us, event | category | flops | bytes accessed | tf_op | source)
XLA Modules:
  0.0 44.9 jit_solution(5889019164970318)
XLA Ops:
  1.3 0.0 copy-start
  1.3 0.0 copy-start.1
  1.3 6.0 %forward.1 = (bf16[8,128,128]{2,1,0:T(8,128)(2,1)S(1)}, s32[1188]{0:T(1024)S(4)}, s32[8]{0:T(128)S(4)}, bf16[256,128,128]{2,1,0:T(8,128)(2,1)S(1)}) custom-call(s32[1]{0:T(128)S(6)} %copy.15.live_count, s32[256]{0:T(256)} %tile_hbm.1, s32[256]{0:T(256)} %slot_hbm.1, s32[8]{0:T(128)} %ray_hbm.1, ...), custom_call_target="tpu_custom_call", output_to_operand_aliasing={{3}: (6, {})} | custom-call | tf_op jit(solution)/shard_map/forward/pallas_call | solution.py:224
  7.3 16.0 %all_to_all.10 = bf16[8,1,128,128]{3,2,1,0:T(8,128)(2,1)S(1)} all-to-all(bf16[8,1,128,128]{3,2,1,0:T(8,128)(2,1)S(1)} %bitcast.15), channel_id=1, replica_groups=mesh['region'=8,'angle'=4] {'region'}, dimensions={0} | all-to-all | bytes 524288 | tf_op jit(solution)/shard_map/all_to_all | solution.py:249
  23.3 0.0 copy-done
  23.3 0.0 copy-done.1
  23.3 0.2 outgoing.1
  23.5 12.6 %all_to_all.11 = bf16[8,1,128,128]{3,2,1,0:T(8,128)(2,1)S(1)} all-to-all(bf16[8,1,128,128]{3,2,1,0:T(8,128)(2,1)S(1)} %bitcast.14), channel_id=1, replica_groups=mesh['region'=8,'angle'=4] {'region'}, dimensions={0} | all-to-all | bytes 524288 | tf_op jit(solution)/shard_map/all_to_all | solution.py:266
  36.1 1.0 %backward_3.1 = bf16[4,128,128]{2,1,0:T(8,128)(2,1)S(1)} custom-call(s32[1188]{0:T(1024)S(4)} %get-tuple-element.13.lists, bf16[256,128,128]{2,1,0:T(8,128)(2,1)S(1)} %get-tuple-element.14.kept, bf16[8,128,128]{2,1,0:T(8,128)(2,1)S(1)} %bitcast.8), custom_call_target="tpu_custom_call" | custom-call | tf_op jit(solution)/shard_map/backward_3/pallas_call | solution.py:275
  37.1 0.1 collective-permute-start
  37.1 1.0 %backward_2.1.share = f32[4,128,128]{2,1,0:T(8,128)S(1)} custom-call(s32[1188]{0:T(1024)S(4)} %get-tuple-element.13.lists, bf16[256,128,128]{2,1,0:T(8,128)(2,1)S(1)} %get-tuple-element.14.kept, bf16[8,128,128]{2,1,0:T(8,128)(2,1)S(1)} %bitcast.9), custom_call_target="tpu_custom_call" | custom-call | tf_op jit(solution)/shard_map/backward_2/pallas_call | solution.py:275
  38.1 0.4 collective-permute-done.refs_0_
  38.5 0.1 collective-permute-start.1
  38.6 1.2 %own.1 = (f32[4,128,128]{2,1,0:T(8,128)S(1)}, f32[4,1,128]{2,1,0:T(1,128)S(1)}, f32[8,128,128]{2,1,0:T(8,128)}) custom-call(s32[1188]{0:T(1024)S(4)} %get-tuple-element.13.lists, s32[8]{0:T(128)S(4)} %get-tuple-element.15.ray_of, bf16[256,128,128]{2,1,0:T(8,128)(2,1)S(1)} %get-tuple-element.14.kept, bf16[8,128,128]{2,1,0:T(8,128)(2,1)S(1)} %bitcast.10, ...), custom_call_target="tpu_custom_call" | custom-call | tf_op jit(solution)/shard_map/own/pallas_call | solution.py:308
  39.8 1.0 %backward_1.1 = bf16[4,128,128]{2,1,0:T(8,128)(2,1)S(1)} custom-call(s32[1188]{0:T(1024)S(4)} %get-tuple-element.13.lists, bf16[256,128,128]{2,1,0:T(8,128)(2,1)S(1)} %get-tuple-element.14.kept, bf16[8,128,128]{2,1,0:T(8,128)(2,1)S(1)} %bitcast.11), custom_call_target="tpu_custom_call" | custom-call | tf_op jit(solution)/shard_map/backward_1/pallas_call | solution.py:275
  40.8 0.2 collective-permute-start.2
  41.0 3.1 %collective-permute-done.1.refs_0_ = bf16[4,128,128]{2,1,0:T(8,128)(2,1)S(1)} collective-permute-done((bf16[4,128,128]{2,1,0:T(8,128)(2,1)S(1)}, bf16[4,128,128]{2,1,0:T(8,128)(2,1)S(1)}, u32[]{:S(2)}, u32[]{:S(2)}) %collective-permute-start.1) | collective-permute-done | bytes 131104 | tf_op jit(solution)/shard_map/ppermute | solution.py:303
  44.1 0.0 collective-permute-done.2.refs_1_
  44.1 0.8 %update.1 = f32[4,128,128]{2,1,0:T(8,128)} custom-call(f32[4,128,128]{2,1,0:T(8,128)S(1)} %get-tuple-element.19.own, f32[4,1,128]{2,1,0:T(1,128)S(1)} %get-tuple-element.20.weight, bf16[4,128,128]{2,1,0:T(8,128)(2,1)S(1)} %collective-permute-done.1.refs_0_, bf16[4,128,128]{2,1,0:T(8,128)(2,1)S(1)} %collective-permute-done.2.refs_1_), custom_call_target="tpu_custom_call" | custom-call | tf_op jit(solution)/shard_map/update/pallas_call | solution.py:331
  (2 shorter events, 0.0 us)
Async XLA Ops:
  1.3 22.0 %copy-start = (f32[8,128,128]{2,1,0:T(8,128)S(1)}, f32[8,128,128]{2,1,0:T(8,128)}, u32[]{:S(2)}) copy-start(f32[8,128,128]{2,1,0:T(8,128)} %sinogram.3) | copy-start | bytes 1572868
  1.3 22.0 %copy-start.1 = (f32[8,128]{1,0:T(8,128)S(1)}, f32[8,128]{1,0:T(8,128)}, u32[]{:S(2)}) copy-start(f32[8,128]{1,0:T(8,128)} %ray_weight.3) | copy-start | bytes 12292
  37.1 1.4 %collective-permute-start = (bf16[4,128,128]{2,1,0:T(8,128)(2,1)S(1)}, bf16[4,128,128]{2,1,0:T(8,128)(2,1)S(1)}, u32[]{:S(2)}, u32[]{:S(2)}) collective-permute-start(bf16[4,128,128]{2,1,0:T(8,128)(2,1)S(1)} %backward_3.1), channel_id=1, source_target_pairs={{0,1},{1,0},{2,3},{3,2},{4,5},{5,4},{6,7},{7,6},{8,9},{9,8},{10,11... | collective-permute-start | bytes 393224 | tf_op jit(solution)/shard_map/ppermute | solution.py:303
  38.5 5.6 %collective-permute-start.1 = (bf16[4,128,128]{2,1,0:T(8,128)(2,1)S(1)}, bf16[4,128,128]{2,1,0:T(8,128)(2,1)S(1)}, u32[]{:S(2)}, u32[]{:S(2)}) collective-permute-start(bf16[4,128,128]{2,1,0:T(8,128)(2,1)S(1)} %join_2.1), channel_id=1, source_target_pairs={{0,2},{1,3},{2,0},{3,1},{4,6},{5,7},{6,4},{7,5},{8,10},{9,11},{10,... | collective-permute-start | bytes 393224 | tf_op jit(solution)/shard_map/ppermute | solution.py:303
  40.8 3.3 %collective-permute-start.2 = (bf16[4,128,128]{2,1,0:T(8,128)(2,1)S(1)}, bf16[4,128,128]{2,1,0:T(8,128)(2,1)S(1)}, u32[]{:S(2)}, u32[]{:S(2)}) collective-permute-start(bf16[4,128,128]{2,1,0:T(8,128)(2,1)S(1)} %backward_1.1), channel_id=1, source_target_pairs={{0,1},{1,0},{2,3},{3,2},{4,5},{5,4},{6,7},{7,6},{8,9},{9,8},{10,11... | collective-permute-start | bytes 393224 | tf_op jit(solution)/shard_map/ppermute | solution.py:303

commit v6 on v5

--- a/solution.py
+++ b/solution.py
@@ -8,7 +8,7 @@
 from jax.sharding import PartitionSpec as P
 
 FORWARD_PARTS = 3
-BACKWARD_PAIRS = 16
+BACKWARD_PAIRS = 12
 SLOT_BIT = 1 << 16
 TILE_BIT = 1 << 24
 VMEM_LIMIT = 24 * 1024 * 1024

time: 44.7 us -> 44.8 us (level); the launches traced: 44.9 us -> 44.1 us
  Pallas kernels: 11.1 us -> 9.73 us
  starting transfers between devices: 0.36 us -> 1.11 us
  waiting for transfers between devices: 3.48 us -> 2.82 us
  blocking collectives: 28.5 us -> 29.1 us
    all_to_all x1, blocking collectives: 16 us -> 17.1 us  [body(): lax.all_to_all(partial_value.reshape((n_region, capacity, slices, rays)),...]
    pallas_call x1, Pallas kernels: 6.01 us -> 4.87 us  [body(): pl.pallas_call(functools.partial(forward_kernel, per_angle, n_angle, room...]
    ppermute x3, starting transfers between devices: 0.36 us -> 1.11 us  [send(): lax.ppermute(share, 'angle', there)]
    ppermute x3, waiting for transfers between devices: 3.48 us -> 2.82 us  [send(): lax.ppermute(share, 'angle', there)]
    all_to_all x1, blocking collectives: 12.6 us -> 12 us  [body(): lax.all_to_all(outgoing.reshape((n_region, capacity, slices, rays)), 'reg...]
    pallas_call x3, Pallas kernels: 2.89 us -> 2.43 us  [backward(): pl.pallas_call(functools.partial(backward_kernel, mask, n_angle), out_sha...]
where the time goes in v6:
time: 44.8 us; the launch traced here: 44.1 us
  blocking collectives  29.1 us (65%)
  Pallas kernels  9.73 us (22%)
  waiting for transfers between devices  2.82 us (6%)
  between operations  1.37 us (3%)
  starting transfers between devices  1.11 us (2%)
    all_to_all x1, blocking collectives, body(): lax.all_to_all(partial_value.reshape((n_region, capacity, slices, rays)),...  17.1 us
    all_to_all x1, blocking collectives, body(): lax.all_to_all(outgoing.reshape((n_region, capacity, slices, rays)), 'reg...  12 us
    pallas_call x1, Pallas kernels, body(): pl.pallas_call(functools.partial(forward_kernel, per_angle, n_angle, room...  4.87 us
    ppermute x3, waiting for transfers between devices, send(): lax.ppermute(share, 'angle', there)  2.82 us
    pallas_call x3, Pallas kernels, backward(): pl.pallas_call(functools.partial(backward_kernel, mask, n_angle), out_sha...  2.43 us
    pallas_call x1, Pallas kernels, body(): pl.pallas_call(functools.partial(own_kernel, n_angle), out_shape=(jax.Sha...  1.43 us
    ppermute x3, starting transfers between devices, send(): lax.ppermute(share, 'angle', there)  1.11 us
  transfers between devices with their start and end apart: 3, of which 2 were waited for; matrix products, arithmetic and copies ran while one was open for 0% of the time, Pallas kernels for 7%

profile of v6, /device:TPU:0, one launch (start us, length us, event | category | flops | bytes accessed | tf_op | source)
XLA Modules:
  0.0 44.1 jit_solution(8416273461340464451)
XLA Ops:
  1.3 0.0 copy-start
  1.3 0.0 copy-start.1
  1.3 4.9 %forward.1 = (bf16[8,128,128]{2,1,0:T(8,128)(2,1)S(1)}, s32[1156]{0:T(1024)S(4)}, s32[8]{0:T(128)S(4)}, bf16[256,128,128]{2,1,0:T(8,128)(2,1)S(1)}) custom-call(s32[1]{0:T(128)S(6)} %copy.15.live_count, s32[256]{0:T(256)} %tile_hbm.1, s32[256]{0:T(256)} %slot_hbm.1, s32[8]{0:T(128)} %ray_hbm.1, ...), custom_call_target="tpu_custom_call", output_to_operand_aliasing={{3}: (6, {})} | custom-call | tf_op jit(solution)/shard_map/forward/pallas_call | solution.py:224
  6.2 17.1 %all_to_all.10 = bf16[8,1,128,128]{3,2,1,0:T(8,128)(2,1)S(1)} all-to-all(bf16[8,1,128,128]{3,2,1,0:T(8,128)(2,1)S(1)} %bitcast.15), channel_id=1, replica_groups=mesh['region'=8,'angle'=4] {'region'}, dimensions={0} | all-to-all | bytes 524288 | tf_op jit(solution)/shard_map/all_to_all | solution.py:249
  23.3 0.0 copy-done
  23.3 0.0 copy-done.1
  23.3 0.2 outgoing.1
  23.5 12.0 %all_to_all.11 = bf16[8,1,128,128]{3,2,1,0:T(8,128)(2,1)S(1)} all-to-all(bf16[8,1,128,128]{3,2,1,0:T(8,128)(2,1)S(1)} %bitcast.14), channel_id=1, replica_groups=mesh['region'=8,'angle'=4] {'region'}, dimensions={0} | all-to-all | bytes 524288 | tf_op jit(solution)/shard_map/all_to_all | solution.py:266
  35.5 0.8 %backward_3.1 = bf16[4,128,128]{2,1,0:T(8,128)(2,1)S(1)} custom-call(s32[1156]{0:T(1024)S(4)} %get-tuple-element.13.lists, bf16[256,128,128]{2,1,0:T(8,128)(2,1)S(1)} %get-tuple-element.14.kept, bf16[8,128,128]{2,1,0:T(8,128)(2,1)S(1)} %bitcast.8), custom_call_target="tpu_custom_call" | custom-call | tf_op jit(solution)/shard_map/backward_3/pallas_call | solution.py:275
  36.3 0.1 collective-permute-start
  36.4 0.8 %backward_2.1.share = f32[4,128,128]{2,1,0:T(8,128)S(1)} custom-call(s32[1156]{0:T(1024)S(4)} %get-tuple-element.13.lists, bf16[256,128,128]{2,1,0:T(8,128)(2,1)S(1)} %get-tuple-element.14.kept, bf16[8,128,128]{2,1,0:T(8,128)(2,1)S(1)} %bitcast.9), custom_call_target="tpu_custom_call" | custom-call | tf_op jit(solution)/shard_map/backward_2/pallas_call | solution.py:275
  37.2 0.5 %collective-permute-done.refs_0_ = bf16[4,128,128]{2,1,0:T(8,128)(2,1)S(1)} collective-permute-done((bf16[4,128,128]{2,1,0:T(8,128)(2,1)S(1)}, bf16[4,128,128]{2,1,0:T(8,128)(2,1)S(1)}, u32[]{:S(2)}, u32[]{:S(2)}) %collective-permute-start) | collective-permute-done | bytes 131104 | tf_op jit(solution)/shard_map/ppermute | solution.py:303
  37.7 1.0 %collective-permute-start.1 = (bf16[4,128,128]{2,1,0:T(8,128)(2,1)S(1)}, bf16[4,128,128]{2,1,0:T(8,128)(2,1)S(1)}, u32[]{:S(2)}, u32[]{:S(2)}) collective-permute-start(bf16[4,128,128]{2,1,0:T(8,128)(2,1)S(1)} %join_2.1), channel_id=1, source_target_pairs={{0,2},{1,3},{2,0},{3,1},{4,6},{5,7},{6,4},{7,5},{8,10},{9,11},{10,... | collective-permute-start | bytes 393224 | tf_op jit(solution)/shard_map/ppermute | solution.py:303
  38.7 1.4 %own.1 = (f32[4,128,128]{2,1,0:T(8,128)S(1)}, f32[4,1,128]{2,1,0:T(1,128)S(1)}, f32[8,128,128]{2,1,0:T(8,128)}) custom-call(s32[1156]{0:T(1024)S(4)} %get-tuple-element.13.lists, s32[8]{0:T(128)S(4)} %get-tuple-element.15.ray_of, bf16[256,128,128]{2,1,0:T(8,128)(2,1)S(1)} %get-tuple-element.14.kept, bf16[8,128,128]{2,1,0:T(8,128)(2,1)S(1)} %bitcast.10, ...), custom_call_target="tpu_custom_call" | custom-call | tf_op jit(solution)/shard_map/own/pallas_call | solution.py:308
  40.1 0.8 %backward_1.1 = bf16[4,128,128]{2,1,0:T(8,128)(2,1)S(1)} custom-call(s32[1156]{0:T(1024)S(4)} %get-tuple-element.13.lists, bf16[256,128,128]{2,1,0:T(8,128)(2,1)S(1)} %get-tuple-element.14.kept, bf16[8,128,128]{2,1,0:T(8,128)(2,1)S(1)} %bitcast.11), custom_call_target="tpu_custom_call" | custom-call | tf_op jit(solution)/shard_map/backward_1/pallas_call | solution.py:275
  41.0 0.1 collective-permute-start.2
  41.0 2.3 %collective-permute-done.1.refs_0_ = bf16[4,128,128]{2,1,0:T(8,128)(2,1)S(1)} collective-permute-done((bf16[4,128,128]{2,1,0:T(8,128)(2,1)S(1)}, bf16[4,128,128]{2,1,0:T(8,128)(2,1)S(1)}, u32[]{:S(2)}, u32[]{:S(2)}) %collective-permute-start.1) | collective-permute-done | bytes 131104 | tf_op jit(solution)/shard_map/ppermute | solution.py:303
  43.4 0.0 collective-permute-done.2.refs_1_
  43.4 0.8 %update.1 = f32[4,128,128]{2,1,0:T(8,128)} custom-call(f32[4,128,128]{2,1,0:T(8,128)S(1)} %get-tuple-element.19.own, f32[4,1,128]{2,1,0:T(1,128)S(1)} %get-tuple-element.20.weight, bf16[4,128,128]{2,1,0:T(8,128)(2,1)S(1)} %collective-permute-done.1.refs_0_, bf16[4,128,128]{2,1,0:T(8,128)(2,1)S(1)} %collective-permute-done.2.refs_1_), custom_call_target="tpu_custom_call" | custom-call | tf_op jit(solution)/shard_map/update/pallas_call | solution.py:331
  (2 shorter events, 0.0 us)
Async XLA Ops:
  1.3 22.0 %copy-start = (f32[8,128,128]{2,1,0:T(8,128)S(1)}, f32[8,128,128]{2,1,0:T(8,128)}, u32[]{:S(2)}) copy-start(f32[8,128,128]{2,1,0:T(8,128)} %sinogram.3) | copy-start | bytes 1572868
  1.3 22.0 %copy-start.1 = (f32[8,128]{1,0:T(8,128)S(1)}, f32[8,128]{1,0:T(8,128)}, u32[]{:S(2)}) copy-start(f32[8,128]{1,0:T(8,128)} %ray_weight.3) | copy-start | bytes 12292
  36.3 1.4 %collective-permute-start = (bf16[4,128,128]{2,1,0:T(8,128)(2,1)S(1)}, bf16[4,128,128]{2,1,0:T(8,128)(2,1)S(1)}, u32[]{:S(2)}, u32[]{:S(2)}) collective-permute-start(bf16[4,128,128]{2,1,0:T(8,128)(2,1)S(1)} %backward_3.1), channel_id=1, source_target_pairs={{0,1},{1,0},{2,3},{3,2},{4,5},{5,4},{6,7},{7,6},{8,9},{9,8},{10,11... | collective-permute-start | bytes 393224 | tf_op jit(solution)/shard_map/ppermute | solution.py:303
  37.7 5.6 %collective-permute-start.1 = (bf16[4,128,128]{2,1,0:T(8,128)(2,1)S(1)}, bf16[4,128,128]{2,1,0:T(8,128)(2,1)S(1)}, u32[]{:S(2)}, u32[]{:S(2)}) collective-permute-start(bf16[4,128,128]{2,1,0:T(8,128)(2,1)S(1)} %join_2.1), channel_id=1, source_target_pairs={{0,2},{1,3},{2,0},{3,1},{4,6},{5,7},{6,4},{7,5},{8,10},{9,11},{10,... | collective-permute-start | bytes 393224 | tf_op jit(solution)/shard_map/ppermute | solution.py:303
  41.0 2.4 %collective-permute-start.2 = (bf16[4,128,128]{2,1,0:T(8,128)(2,1)S(1)}, bf16[4,128,128]{2,1,0:T(8,128)(2,1)S(1)}, u32[]{:S(2)}, u32[]{:S(2)}) collective-permute-start(bf16[4,128,128]{2,1,0:T(8,128)(2,1)S(1)} %backward_1.1), channel_id=1, source_target_pairs={{0,1},{1,0},{2,3},{3,2},{4,5},{5,4},{6,7},{7,6},{8,9},{9,8},{10,11... | collective-permute-start | bytes 393224 | tf_op jit(solution)/shard_map/ppermute | solution.py:303
